TPU v7x, 512 devices: a whole 4x8x8 slice. The times are simulated.
512 devices in a mesh: tile: 128 (over y, z_hi, x, core), mp: 4 (over z_lo).
Axes of the slice: x: 4, y: 8, z: 8 (z_hi: 2, z_lo: 4; z = z_hi * 4 + z_lo), core: 2. Of those that a mesh axis runs over, the one named last changes fastest.
Arguments:
- query: bfloat16 [32768, 1536], P('tile', 'mp'), may hold values from -28 to 28
- key: bfloat16 [32768, 1536], P('tile', 'mp'), may hold values from -6 to 6
- value: bfloat16 [32768, 1536], P('tile', 'mp'), may hold values from -6 to 6
- grad_y: bfloat16 [32768, 3072], P('tile', 'mp'), may hold values from -12 to 12
- w_out: bfloat16 [3072, 1536], P('tile', 'mp'), may hold values from -0.109375 to 0.109375
Outputs:
- grad_query: bfloat16 [32768, 1536], P('tile', 'mp')
- grad_key: bfloat16 [32768, 1536], P('tile', 'mp')
- grad_value: bfloat16 [32768, 1536], P('tile', 'mp')
All inputs are finite; a program needn't handle non-finite values.
Results may differ from a plain program's by a relative error of at most 0.0095.
Values may be sent and summed in bfloat16 or wider, within the bound.
A program may use at most 64 MiB of HBM per device.

v0:
```python
import jax
import jax.numpy as jnp
from jax import lax
from jax.sharding import PartitionSpec as P

HD = 128
BAND = 8
TILE_COLS = 8
TH = 16
TW = 16


def passed_along(value, axis, by):
    devices = lax.axis_size(axis)
    pairs = [(i, i + by) for i in range(devices) if 0 <= i + by < devices]
    return lax.ppermute(value, axis, pairs)


def source_span(offset, length, margin):
    if offset < 0:
        return (length - margin, margin)
    if offset == 0:
        return (0, length)
    return (0, margin)


def window_span(offset, length, margin):
    if offset < 0:
        return (0, margin)
    if offset == 0:
        return (margin, length)
    return (margin + length, margin)


def shards(query, key, value, grad_y, w_out):
    tokens_dev = query.shape[0]
    feat_dev = query.shape[1]
    columns = TILE_COLS
    grid_rows = lax.axis_size("tile") // columns
    tile_index = lax.axis_index("tile")
    tile_row = tile_index // columns
    tile_col = tile_index % columns
    full_grad = lax.all_gather(grad_y, "mp", axis=1, tiled=True)
    cotangent = jnp.dot(
        full_grad,
        lax.all_gather(w_out, "tile", axis=0, tiled=True),
        preferred_element_type=jnp.float32,
    ).astype(jnp.bfloat16)
    key_value = jnp.stack([key, value]).reshape(2, TH, TW, feat_dev)
    window_rows = TH + 2 * BAND
    window_cols = TW + 2 * BAND
    neighbours = [(-1, -1), (-1, 0), (-1, 1), (0, -1), (0, 1), (1, -1), (1, 0), (1, 1)]
    strips = []
    for row_offset in (-1, 0, 1):
        pieces = []
        for col_offset in (-1, 0, 1):
            row_begin, row_extent = source_span(row_offset, TH, BAND)
            col_begin, col_extent = source_span(col_offset, TW, BAND)
            fragment = key_value[
                :, row_begin : row_begin + row_extent, col_begin : col_begin + col_extent
            ]
            if row_offset != 0 or col_offset != 0:
                fragment = passed_along(fragment, "tile", -(row_offset * columns + col_offset))
            pieces.append(fragment)
        strips.append(jnp.concatenate(pieces, axis=2))
    window = jnp.concatenate(strips, axis=1)
    row_iota = lax.broadcasted_iota(jnp.int32, (window_rows, window_cols), 0)
    col_iota = lax.broadcasted_iota(jnp.int32, (window_rows, window_cols), 1)
    row_valid = ((row_iota >= BAND) | (tile_row > 0)) & (
        (row_iota < BAND + TH) | (tile_row < grid_rows - 1)
    )
    col_valid = ((col_iota >= BAND) | (tile_col > 0)) & (
        (col_iota < BAND + TW) | (tile_col < columns - 1)
    )
    key_valid = (row_valid & col_valid).reshape(-1)
    keys_win = window[0].reshape(window_rows * window_cols, feat_dev)
    values_win = window[1].reshape(window_rows * window_cols, feat_dev)
    score_scale = HD ** (-0.5)
    contract_last = (((1,), (1,)), ((), ()))
    contract_first = (((0,), (0,)), ((), ()))
    query_grads = []
    key_grads = []
    value_grads = []
    for head_index in range(feat_dev // HD):
        column_start = head_index * HD
        query_head = query[:, column_start : column_start + HD]
        key_head = keys_win[:, column_start : column_start + HD]
        value_head = values_win[:, column_start : column_start + HD]
        cotan_head = cotangent[:, column_start : column_start + HD]
        scores = (
            lax.dot_general(query_head, key_head, contract_last, preferred_element_type=jnp.float32)
            * score_scale
        )
        scores = jnp.where(key_valid[None, :], scores, -jnp.inf)
        row_peak = jnp.max(scores, axis=-1, keepdims=True)
        unnormed = jnp.exp(scores - row_peak)
        attention = unnormed / jnp.sum(unnormed, axis=-1, keepdims=True)
        attention_low = attention.astype(jnp.bfloat16)
        grad_attention = lax.dot_general(
            cotan_head, value_head, contract_last, preferred_element_type=jnp.float32
        )
        row_total = jnp.sum(attention * grad_attention, axis=-1, keepdims=True)
        grad_scores = (attention * (grad_attention - row_total) * score_scale).astype(jnp.bfloat16)
        query_grads.append(jnp.dot(grad_scores, key_head, preferred_element_type=jnp.float32))
        key_grads.append(
            lax.dot_general(
                grad_scores, query_head, contract_first, preferred_element_type=jnp.float32
            )
        )
        value_grads.append(
            lax.dot_general(
                attention_low, cotan_head, contract_first, preferred_element_type=jnp.float32
            )
        )
    grad_query = jnp.concatenate(query_grads, axis=1).astype(jnp.bfloat16)
    grad_window = jnp.stack(
        [jnp.concatenate(key_grads, axis=1), jnp.concatenate(value_grads, axis=1)]
    )
    grad_window = grad_window.reshape(2, window_rows, window_cols, feat_dev)
    center = grad_window[:, BAND : BAND + TH, BAND : BAND + TW]
    for row_offset, col_offset in neighbours:
        row_begin, row_extent = window_span(row_offset, TH, BAND)
        col_begin, col_extent = window_span(col_offset, TW, BAND)
        fragment = grad_window[
            :, row_begin : row_begin + row_extent, col_begin : col_begin + col_extent
        ]
        arrived = passed_along(
            fragment.astype(jnp.bfloat16), "tile", row_offset * columns + col_offset
        ).astype(fragment.dtype)
        row_target, row_target_extent = source_span(row_offset, TH, BAND)
        col_target, col_target_extent = source_span(col_offset, TW, BAND)
        center = center.at[
            :,
            row_target : row_target + row_target_extent,
            col_target : col_target + col_target_extent,
        ].add(arrived)
    gradients = center.reshape(2, tokens_dev, feat_dev).astype(jnp.bfloat16)
    return (grad_query, gradients[0], gradients[1])


def solution(mesh):
    return jax.shard_map(
        shards,
        mesh=mesh,
        in_specs=(
            P("tile", "mp"),
            P("tile", "mp"),
            P("tile", "mp"),
            P("tile", "mp"),
            P("tile", "mp"),
        ),
        out_specs=(P("tile", "mp"), P("tile", "mp"), P("tile", "mp")),
        check_vma=False,
    )
```

profile of v0, /device:TPU:57, one launch (start us, length us, event | category | flops | bytes accessed | tf_op | source)
XLA Modules:
  0.0 298.0 jit_solution(5893653378903548960)
XLA Ops:
  7.2 0.7 all-gather.3.cloned.1.call-update
  8.0 0.7 all-gather.5.cloned.1.call-update
  8.7 1.0 fusion.46
  9.7 12.0 %collective-permute-start.7 = (bf16[2,8,8,384]{3,2,1,0:T(8,128)(2,1)S(1)}, bf16[2,8,8,384]{3,2,1,0:T(8,128)(2,1)S(1)}, u32[]{:S(2)}, u32[]{:S(2)}) collective-permute-start(bf16[2,8,8,384]{3,2,1,0:T(8,128)(2,1)S(1)} %get-tuple-element.124), channel_id=1, source_target_pairs={{36,0},{40,4},{44,8},{48,12},{52,16},{56,20},{60,24},{64,28},{68,3... | collective-permute-start | bytes 294920 | tf_op jit(solution)/shard_map/ppermute | solution.py:16
  21.7 1.1 fusion.41
  22.8 1.9 collective-permute-start.6
  24.7 9.0 %collective-permute-start.5 = (bf16[2,8,8,384]{3,2,1,0:T(8,128)(2,1)S(1)}, bf16[2,8,8,384]{3,2,1,0:T(8,128)(2,1)S(1)}, u32[]{:S(2)}, u32[]{:S(2)}) collective-permute-start(bf16[2,8,8,384]{3,2,1,0:T(8,128)(2,1)S(1)} %get-tuple-element.123), channel_id=1, source_target_pairs={{28,0},{32,4},{36,8},{40,12},{44,16},{48,20},{52,24},{56,28},{60,3... | collective-permute-start | bytes 294920 | tf_op jit(solution)/shard_map/ppermute | solution.py:16
  33.7 1.9 collective-permute-start.4
  35.7 3.6 %collective-permute-start.3 = (bf16[2,16,8,384]{3,2,1,0:T(8,128)(2,1)S(1)}, bf16[2,16,8,384]{3,2,1,0:T(8,128)(2,1)S(1)}, u32[]{:S(2)}, u32[]{:S(2)}) collective-permute-start(bf16[2,16,8,384]{3,2,1,0:T(8,128)(2,1)S(1)} %get-tuple-element.127), channel_id=1, source_target_pairs={{0,4},{4,8},{8,12},{12,16},{16,20},{20,24},{24,28},{28,32},{32,36}... | collective-permute-start | bytes 589832 | tf_op jit(solution)/shard_map/ppermute | solution.py:16
  39.5 4.4 %collective-permute-start.2 = (bf16[2,8,8,384]{3,2,1,0:T(8,128)(2,1)S(1)}, bf16[2,8,8,384]{3,2,1,0:T(8,128)(2,1)S(1)}, u32[]{:S(2)}, u32[]{:S(2)}) collective-permute-start(bf16[2,8,8,384]{3,2,1,0:T(8,128)(2,1)S(1)} %get-tuple-element.122), channel_id=1, source_target_pairs={{0,28},{4,32},{8,36},{12,40},{16,44},{20,48},{24,52},{28,56},{32,6... | collective-permute-start | bytes 294920 | tf_op jit(solution)/shard_map/ppermute | solution.py:16
  44.0 1.9 collective-permute-start.1
  45.9 0.7 and_reduce_fusion
  46.6 6.3 %collective-permute-done.2 = bf16[2,8,8,384]{3,2,1,0:T(8,128)(2,1)S(1)} collective-permute-done((bf16[2,8,8,384]{3,2,1,0:T(8,128)(2,1)S(1)}, bf16[2,8,8,384]{3,2,1,0:T(8,128)(2,1)S(1)}, u32[]{:S(2)}, u32[]{:S(2)}) %collective-permute-start.2) | collective-permute-done | bytes 98336 | tf_op jit(solution)/shard_map/ppermute | solution.py:16
  53.0 4.4 %collective-permute-start = (bf16[2,8,8,384]{3,2,1,0:T(8,128)(2,1)S(1)}, bf16[2,8,8,384]{3,2,1,0:T(8,128)(2,1)S(1)}, u32[]{:S(2)}, u32[]{:S(2)}) collective-permute-start(bf16[2,8,8,384]{3,2,1,0:T(8,128)(2,1)S(1)} %get-tuple-element.121), channel_id=1, source_target_pairs={{0,36},{4,40},{8,44},{12,48},{16,52},{20,56},{24,60},{28,64},{32,6... | collective-permute-start | bytes 294920 | tf_op jit(solution)/shard_map/ppermute | solution.py:16
  57.4 0.6 fusion.72
  58.0 9.5 %collective-permute-done = bf16[2,8,8,384]{3,2,1,0:T(8,128)(2,1)S(1)} collective-permute-done((bf16[2,8,8,384]{3,2,1,0:T(8,128)(2,1)S(1)}, bf16[2,8,8,384]{3,2,1,0:T(8,128)(2,1)S(1)}, u32[]{:S(2)}, u32[]{:S(2)}) %collective-permute-start) | collective-permute-done | bytes 98336 | tf_op jit(solution)/shard_map/ppermute | solution.py:16
  67.6 0.8 maximum_maximum_fusion
  68.4 1.0 fusion.70
  69.5 0.4 fusion.73
  70.0 0.4 fusion.74
  70.6 0.4 fusion.75
  71.2 6.3 %all-gather.3.cloned.1.call-done = bf16[256,3072]{1,0:T(8,128)(2,1)} async-done(((bf16[256,768]{1,0:T(8,128)(2,1)}), bf16[256,3072]{1,0:T(8,128)(2,1)}) %all-gather.3.cloned.1.call-update) | async-done | bytes 1572880 | tf_op jit(solution)/shard_map/all_gather | solution.py:43
  77.6 143.1 %all-gather.5.cloned.1.call-done = bf16[3072,384]{1,0:T(8,128)(2,1)} async-done(((bf16[24,384]{1,0:T(8,128)(2,1)}), bf16[3072,384]{1,0:T(8,128)(2,1)}) %all-gather.5.cloned.1.call-update) | async-done | bytes 2359312 | tf_op jit(solution)/shard_map/all_gather | solution.py:46
  220.7 3.2 %convolution_convert_fusion = bf16[256,384]{1,0:T(8,128)(2,1)S(1)} fusion(bf16[256,3072]{1,0:T(8,128)(2,1)} %all-gather.3.cloned.1.call-done, bf16[3072,384]{1,0:T(8,128)(2,1)} %all-gather.5.cloned.1.call-done), kind=kOutput, calls=%fused_computation.15 | convolution fusion | flops 604078080 | bytes 4128768 | tf_op jit(solution)/shard_map/dot_general | solution.py:44
  223.9 0.4 fusion.4
  224.3 0.3 fusion.6
  224.5 0.8 copy-done.4
  225.4 0.9 convolution_convert_fusion.1
  226.3 0.3 fusion.55
  226.6 0.4 fusion.7
  227.0 0.3 fusion.9
  227.3 0.9 convolution_convert_fusion.2
  228.2 0.3 fusion.58
  228.5 0.4 fusion.10
  228.9 0.3 fusion.12
  229.1 0.9 convolution_convert_fusion.3
  230.0 0.3 fusion.61
  230.4 1.2 fusion.22
  231.5 1.1 fusion.21
  232.7 1.2 fusion.20
  234.0 0.5 copy.23
  234.5 2.7 pad_maximum_fusion.2
  237.2 1.9 copy.24
  239.3 0.8 fusion.67
  240.1 0.7 fusion.68
  240.8 0.8 fusion.69
  241.6 0.8 copy.25
  242.4 1.9 collective-permute-start.8
  244.4 7.5 %collective-permute-start.9 = (bf16[2,8,16,384]{3,2,1,0:T(8,128)(2,1)}, bf16[2,8,16,384]{3,2,1,0:T(8,128)(2,1)S(1)}, u32[]{:S(2)}, u32[]{:S(2)}) collective-permute-start(bf16[2,8,16,384]{3,2,1,0:T(8,128)(2,1)} %get-tuple-element.114), channel_id=1, source_target_pairs={{32,0},{36,4},{40,8},{44,12},{48,16},{52,20},{56,24},{60,28},{64,3... | collective-permute-start | bytes 589832 | tf_op jit(solution)/shard_map/ppermute | solution.py:16
  251.9 3.1 %collective-permute-start.10 = (bf16[2,8,8,384]{3,2,1,0:T(8,128)(2,1)}, bf16[2,8,8,384]{3,2,1,0:T(8,128)(2,1)S(1)}, u32[]{:S(2)}, u32[]{:S(2)}) collective-permute-start(bf16[2,8,8,384]{3,2,1,0:T(8,128)(2,1)} %get-tuple-element.111), channel_id=1, source_target_pairs={{28,0},{32,4},{36,8},{40,12},{44,16},{48,20},{52,24},{56,28},{60,3... | collective-permute-start | bytes 294920 | tf_op jit(solution)/shard_map/ppermute | solution.py:16
  255.0 1.9 collective-permute-start.11
  256.9 3.8 %collective-permute-start.12 = (bf16[2,16,8,384]{3,2,1,0:T(8,128)(2,1)}, bf16[2,16,8,384]{3,2,1,0:T(8,128)(2,1)S(1)}, u32[]{:S(2)}, u32[]{:S(2)}) collective-permute-start(bf16[2,16,8,384]{3,2,1,0:T(8,128)(2,1)} %get-tuple-element.115), channel_id=1, source_target_pairs={{0,4},{4,8},{8,12},{12,16},{16,20},{20,24},{24,28},{28,32},{32,36}... | collective-permute-start | bytes 589832 | tf_op jit(solution)/shard_map/ppermute | solution.py:16
  260.8 6.8 %collective-permute-start.13 = (bf16[2,8,8,384]{3,2,1,0:T(8,128)(2,1)S(1)}, bf16[2,8,8,384]{3,2,1,0:T(8,128)(2,1)S(1)}, u32[]{:S(2)}, u32[]{:S(2)}) collective-permute-start(bf16[2,8,8,384]{3,2,1,0:T(8,128)(2,1)S(1)} %copy-done.7), channel_id=1, source_target_pairs={{0,28},{4,32},{8,36},{12,40},{16,44},{20,48},{24,52},{28,56},{32,6... | collective-permute-start | bytes 294920 | tf_op jit(solution)/shard_map/ppermute | solution.py:16
  267.6 1.9 collective-permute-start.14
  269.7 1.9 collective-permute-start.15
  271.8 2.0 collective-permute-done.13
  273.8 1.9 add_select_fusion
  275.7 2.9 scatter-add.35
  278.6 1.5 collective-permute-done.14
  280.1 1.8 constant_dynamic-update-slice_fusion
  281.9 6.6 %collective-permute-done.15 = bf16[2,8,8,384]{3,2,1,0:T(8,128)(2,1)S(1)} collective-permute-done((bf16[2,8,8,384]{3,2,1,0:T(8,128)(2,1)}, bf16[2,8,8,384]{3,2,1,0:T(8,128)(2,1)S(1)}, u32[]{:S(2)}, u32[]{:S(2)}) %collective-permute-start.15) | collective-permute-done | bytes 98336 | tf_op jit(solution)/shard_map/ppermute | solution.py:16
  288.5 0.7 fusion.44
  289.2 1.2 convert_element_type.73
  290.4 0.8 fusion.71
  (53 shorter events, 1.9 us)
Async XLA Ops:
  7.2 38.7 %copy-start.11 = (s32[4]{0:T(128)S(1)}, s32[4]{0:T(128)}, u32[]{:S(2)}) copy-start(s32[4]{0:T(128)} %constant.262.clone.1) | copy-start | bytes 52
  7.2 26.5 %copy-start.1 = (bf16[256,384]{1,0:T(8,128)(2,1)S(1)}, bf16[256,384]{1,0:T(8,128)(2,1)}, u32[]{:S(2)}) copy-start(bf16[256,384]{1,0:T(8,128)(2,1)} %param.22) | copy-start | bytes 589828
  7.2 26.5 %copy-start.2 = (bf16[256,384]{1,0:T(8,128)(2,1)S(1)}, bf16[256,384]{1,0:T(8,128)(2,1)}, u32[]{:S(2)}) copy-start(bf16[256,384]{1,0:T(8,128)(2,1)} %param.23) | copy-start | bytes 589828
  7.2 70.4 %all-gather.3.cloned.1.call-start = ((), (), s32[]{:S(2)}) async-start(), calls=%async_computation | async-start | bytes 1966080 | tf_op jit(solution)/shard_map/all_gather | solution.py:43
  7.9 212.7 %all-gather.5.cloned.1.call-start = ((), (), s32[]{:S(2)}) async-start(), calls=%async_computation.1 | async-start | bytes 2377728 | tf_op jit(solution)/shard_map/all_gather | solution.py:46
  9.7 29.8 %collective-permute-start.7 = (bf16[2,8,8,384]{3,2,1,0:T(8,128)(2,1)S(1)}, bf16[2,8,8,384]{3,2,1,0:T(8,128)(2,1)S(1)}, u32[]{:S(2)}, u32[]{:S(2)}) collective-permute-start(bf16[2,8,8,384]{3,2,1,0:T(8,128)(2,1)S(1)} %get-tuple-element.124), channel_id=1, source_target_pairs={{36,0},{40,4},{44,8},{48,12},{52,16},{56,20},{60,24},{64,28},{68,3... | collective-permute-start | bytes 294920 | tf_op jit(solution)/shard_map/ppermute | solution.py:16
  22.8 44.8 %collective-permute-start.6 = (bf16[2,8,16,384]{3,2,1,0:T(8,128)(2,1)S(1)}, bf16[2,8,16,384]{3,2,1,0:T(8,128)(2,1)S(1)}, u32[]{:S(2)}, u32[]{:S(2)}) collective-permute-start(bf16[2,8,16,384]{3,2,1,0:T(8,128)(2,1)S(1)} %get-tuple-element.126), channel_id=1, source_target_pairs={{32,0},{36,4},{40,8},{44,12},{48,16},{52,20},{56,24},{60,28},{64,3... | collective-permute-start | bytes 589832 | tf_op jit(solution)/shard_map/ppermute | solution.py:16
  24.7 19.3 %collective-permute-start.5 = (bf16[2,8,8,384]{3,2,1,0:T(8,128)(2,1)S(1)}, bf16[2,8,8,384]{3,2,1,0:T(8,128)(2,1)S(1)}, u32[]{:S(2)}, u32[]{:S(2)}) collective-permute-start(bf16[2,8,8,384]{3,2,1,0:T(8,128)(2,1)S(1)} %get-tuple-element.123), channel_id=1, source_target_pairs={{28,0},{32,4},{36,8},{40,12},{44,16},{48,20},{52,24},{56,28},{60,3... | collective-permute-start | bytes 294920 | tf_op jit(solution)/shard_map/ppermute | solution.py:16
  33.7 33.8 %collective-permute-start.4 = (bf16[2,16,8,384]{3,2,1,0:T(8,128)(2,1)S(1)}, bf16[2,16,8,384]{3,2,1,0:T(8,128)(2,1)S(1)}, u32[]{:S(2)}, u32[]{:S(2)}) collective-permute-start(bf16[2,16,8,384]{3,2,1,0:T(8,128)(2,1)S(1)} %get-tuple-element.128), channel_id=1, source_target_pairs={{4,0},{8,4},{12,8},{16,12},{20,16},{24,20},{28,24},{32,28},{36,32}... | collective-permute-start | bytes 589832 | tf_op jit(solution)/shard_map/ppermute | solution.py:16
  35.7 31.9 %collective-permute-start.3 = (bf16[2,16,8,384]{3,2,1,0:T(8,128)(2,1)S(1)}, bf16[2,16,8,384]{3,2,1,0:T(8,128)(2,1)S(1)}, u32[]{:S(2)}, u32[]{:S(2)}) collective-permute-start(bf16[2,16,8,384]{3,2,1,0:T(8,128)(2,1)S(1)} %get-tuple-element.127), channel_id=1, source_target_pairs={{0,4},{4,8},{8,12},{12,16},{16,20},{20,24},{24,28},{28,32},{32,36}... | collective-permute-start | bytes 589832 | tf_op jit(solution)/shard_map/ppermute | solution.py:16
  39.5 13.4 %collective-permute-start.2 = (bf16[2,8,8,384]{3,2,1,0:T(8,128)(2,1)S(1)}, bf16[2,8,8,384]{3,2,1,0:T(8,128)(2,1)S(1)}, u32[]{:S(2)}, u32[]{:S(2)}) collective-permute-start(bf16[2,8,8,384]{3,2,1,0:T(8,128)(2,1)S(1)} %get-tuple-element.122), channel_id=1, source_target_pairs={{0,28},{4,32},{8,36},{12,40},{16,44},{20,48},{24,52},{28,56},{32,6... | collective-permute-start | bytes 294920 | tf_op jit(solution)/shard_map/ppermute | solution.py:16
  44.0 23.6 %collective-permute-start.1 = (bf16[2,8,16,384]{3,2,1,0:T(8,128)(2,1)S(1)}, bf16[2,8,16,384]{3,2,1,0:T(8,128)(2,1)S(1)}, u32[]{:S(2)}, u32[]{:S(2)}) collective-permute-start(bf16[2,8,16,384]{3,2,1,0:T(8,128)(2,1)S(1)} %get-tuple-element.125), channel_id=1, source_target_pairs={{0,32},{4,36},{8,40},{12,44},{16,48},{20,52},{24,56},{28,60},{32,6... | collective-permute-start | bytes 589832 | tf_op jit(solution)/shard_map/ppermute | solution.py:16
  53.0 14.6 %collective-permute-start = (bf16[2,8,8,384]{3,2,1,0:T(8,128)(2,1)S(1)}, bf16[2,8,8,384]{3,2,1,0:T(8,128)(2,1)S(1)}, u32[]{:S(2)}, u32[]{:S(2)}) collective-permute-start(bf16[2,8,8,384]{3,2,1,0:T(8,128)(2,1)S(1)} %get-tuple-element.121), channel_id=1, source_target_pairs={{0,36},{4,40},{8,44},{12,48},{16,52},{20,56},{24,60},{28,64},{32,6... | collective-permute-start | bytes 294920 | tf_op jit(solution)/shard_map/ppermute | solution.py:16
  68.4 1.1 copy-start.6
  69.5 1.2 copy-start.3
  220.7 3.2 %copy-start.5 = (bf16[1,32,32,384]{3,2,1,0:T(8,128)(2,1)S(1)}, bf16[1,32,32,384]{3,2,1,0:T(8,128)(2,1)}, u32[]{:S(2)}) copy-start(bf16[1,32,32,384]{3,2,1,0:T(8,128)(2,1)} %get-tuple-element.118) | copy-start | bytes 2359300
  224.3 1.1 copy-start.4
  239.3 2.3 copy-start.8
  239.3 2.3 copy-start.9
  239.3 2.3 copy-start.10
  242.4 18.3 %collective-permute-start.8 = (bf16[2,8,8,384]{3,2,1,0:T(8,128)(2,1)}, bf16[2,8,8,384]{3,2,1,0:T(8,128)(2,1)S(1)}, u32[]{:S(2)}, u32[]{:S(2)}) collective-permute-start(bf16[2,8,8,384]{3,2,1,0:T(8,128)(2,1)} %get-tuple-element.112), channel_id=1, source_target_pairs={{36,0},{40,4},{44,8},{48,12},{52,16},{56,20},{60,24},{64,28},{68,3... | collective-permute-start | bytes 294920 | tf_op jit(solution)/shard_map/ppermute | solution.py:16
  244.4 23.2 %collective-permute-start.9 = (bf16[2,8,16,384]{3,2,1,0:T(8,128)(2,1)}, bf16[2,8,16,384]{3,2,1,0:T(8,128)(2,1)S(1)}, u32[]{:S(2)}, u32[]{:S(2)}) collective-permute-start(bf16[2,8,16,384]{3,2,1,0:T(8,128)(2,1)} %get-tuple-element.114), channel_id=1, source_target_pairs={{32,0},{36,4},{40,8},{44,12},{48,16},{52,20},{56,24},{60,28},{64,3... | collective-permute-start | bytes 589832 | tf_op jit(solution)/shard_map/ppermute | solution.py:16
  251.9 17.8 %collective-permute-start.10 = (bf16[2,8,8,384]{3,2,1,0:T(8,128)(2,1)}, bf16[2,8,8,384]{3,2,1,0:T(8,128)(2,1)S(1)}, u32[]{:S(2)}, u32[]{:S(2)}) collective-permute-start(bf16[2,8,8,384]{3,2,1,0:T(8,128)(2,1)} %get-tuple-element.111), channel_id=1, source_target_pairs={{28,0},{32,4},{36,8},{40,12},{44,16},{48,20},{52,24},{56,28},{60,3... | collective-permute-start | bytes 294920 | tf_op jit(solution)/shard_map/ppermute | solution.py:16
  255.0 16.6 %collective-permute-start.11 = (bf16[2,16,8,384]{3,2,1,0:T(8,128)(2,1)}, bf16[2,16,8,384]{3,2,1,0:T(8,128)(2,1)S(1)}, u32[]{:S(2)}, u32[]{:S(2)}) collective-permute-start(bf16[2,16,8,384]{3,2,1,0:T(8,128)(2,1)} %get-tuple-element.116), channel_id=1, source_target_pairs={{4,0},{8,4},{12,8},{16,12},{20,16},{24,20},{28,24},{32,28},{36,32}... | collective-permute-start | bytes 589832 | tf_op jit(solution)/shard_map/ppermute | solution.py:16
  256.9 3.9 %copy-start.7 = (bf16[2,8,8,384]{3,2,1,0:T(8,128)(2,1)S(1)}, bf16[2,8,8,384]{3,2,1,0:T(8,128)(2,1)}, u32[]{:S(2)}) copy-start(bf16[2,8,8,384]{3,2,1,0:T(8,128)(2,1)} %get-tuple-element.110) | copy-start | bytes 294916
  256.9 14.8 %collective-permute-start.12 = (bf16[2,16,8,384]{3,2,1,0:T(8,128)(2,1)}, bf16[2,16,8,384]{3,2,1,0:T(8,128)(2,1)S(1)}, u32[]{:S(2)}, u32[]{:S(2)}) collective-permute-start(bf16[2,16,8,384]{3,2,1,0:T(8,128)(2,1)} %get-tuple-element.115), channel_id=1, source_target_pairs={{0,4},{4,8},{8,12},{12,16},{16,20},{20,24},{24,28},{28,32},{32,36}... | collective-permute-start | bytes 589832 | tf_op jit(solution)/shard_map/ppermute | solution.py:16
  260.8 13.0 %collective-permute-start.13 = (bf16[2,8,8,384]{3,2,1,0:T(8,128)(2,1)S(1)}, bf16[2,8,8,384]{3,2,1,0:T(8,128)(2,1)S(1)}, u32[]{:S(2)}, u32[]{:S(2)}) collective-permute-start(bf16[2,8,8,384]{3,2,1,0:T(8,128)(2,1)S(1)} %copy-done.7), channel_id=1, source_target_pairs={{0,28},{4,32},{8,36},{12,40},{16,44},{20,48},{24,52},{28,56},{32,6... | collective-permute-start | bytes 294920 | tf_op jit(solution)/shard_map/ppermute | solution.py:16
  267.6 12.5 %collective-permute-start.14 = (bf16[2,8,16,384]{3,2,1,0:T(8,128)(2,1)S(1)}, bf16[2,8,16,384]{3,2,1,0:T(8,128)(2,1)S(1)}, u32[]{:S(2)}, u32[]{:S(2)}) collective-permute-start(bf16[2,8,16,384]{3,2,1,0:T(8,128)(2,1)S(1)} %get-tuple-element.113), channel_id=1, source_target_pairs={{0,32},{4,36},{8,40},{12,44},{16,48},{20,52},{24,56},{28,60},{32,6... | collective-permute-start | bytes 589832 | tf_op jit(solution)/shard_map/ppermute | solution.py:16
  269.7 18.9 %collective-permute-start.15 = (bf16[2,8,8,384]{3,2,1,0:T(8,128)(2,1)}, bf16[2,8,8,384]{3,2,1,0:T(8,128)(2,1)S(1)}, u32[]{:S(2)}, u32[]{:S(2)}) collective-permute-start(bf16[2,8,8,384]{3,2,1,0:T(8,128)(2,1)} %get-tuple-element.109), channel_id=1, source_target_pairs={{0,36},{4,40},{8,44},{12,48},{16,52},{20,56},{24,60},{28,64},{32,6... | collective-permute-start | bytes 294920 | tf_op jit(solution)/shard_map/ppermute | solution.py:16
  271.8 2.0 copy-start
Sparse Core Ops, SparseCore 0:
  10.1 67.3 all-gather.2
  82.1 138.4 all-gather.4
where the time goes:
time: 301 us; the launch traced here: 298 us
  waiting for transfers between devices  177 us (59%)
  starting transfers between devices  68.1 us (23%)
  between operations  14.6 us (5%)
  other arithmetic  14.3 us (5%)
  matrix products  12.5 us (4%)
  local copies, waits for them, and re-layouts  11.8 us (4%)
    all_gather x1, waiting for transfers between devices, shards(): lax.all_gather(w_out, 'tile', axis=0, tiled=True)  143 us
    ppermute x16, starting transfers between devices, passed_along(): return lax.ppermute(value, axis, pairs)  68 us
    ppermute x16, waiting for transfers between devices, passed_along(): return lax.ppermute(value, axis, pairs)  26 us
    all_gather x1, waiting for transfers between devices, shards(): full_grad = lax.all_gather(grad_y, 'mp', axis=1, tiled=True)  6.34 us
  transfers between devices with their start and end apart: 18, of which 7 were waited for; matrix products, arithmetic and copies ran while one was open for 5% of the time, Pallas kernels for 0%

commit v1 on v0

v1 whole, which is shorter than its diff:
```python
import jax
import jax.numpy as jnp
from jax import lax
from jax.experimental import pallas as pl
from jax.experimental.pallas import tpu as pltpu
from jax.sharding import PartitionSpec as P

HD = 128
HEADS_DEV = 3
COLUMNS = 8
ROWS = 16
NY = 8
NX = 4
TOK = 256
STRIP = 64
KEYS = 1024
CHUNK = 128
K_DEV = 768
LOG2E = 1.4426950408889634
SCALE = HD ** (-0.5)
MESH = pl.DeviceIdType.MESH
LAST = (((1,), (1,)), ((), ()))
FIRST = (((0,), (0,)), ((), ()))


def tile_of(x, y, z_hi, core):
    return ((y * 2 + z_hi) * NX + x) * 2 + core


def held_block(y, mp):
    p = lax.rem(y - 2 * mp + 2 * NY, NY)
    upper = (p >= 1) & (p <= 4)
    parity = jnp.where(upper, 1, 0)
    idx = jnp.where(upper, p - 1, lax.rem(NY - p, NY))
    return parity, idx // 2, lax.rem(idx, 2)


def to_halves(tokens):
    wide = tokens.astype(jnp.float32).reshape(16, 2, 8, HD)
    return [wide[:, i].reshape(128, HD).astype(jnp.bfloat16) for i in range(2)]


def kernel(
    q_ref, k_ref, v_ref, g_ref, w_ref, dq_ref, dk_ref, dv_ref,
    win, wpad, stage, wbuf, gpair, part, arrived, bias, prob, grad_s, prob_low, dwin,
    ew_out, ew_in, ns_out, ns_in,
    kvns_s, kvns_r, kvew_s, kvew_r, wsc_s, wsc_r, g_s, g_r, wy_s, wy_r, wx_s, wx_r,
    rs_s, rs_r, dew_s, dew_r, dns_s, dns_r,
):
    t = lax.axis_index("tile")
    mp = lax.axis_index("mp")
    core = lax.rem(t, 2)
    x = lax.rem(t // 2, NX)
    z_hi = lax.rem(t // COLUMNS, 2)
    y = t // (2 * COLUMNS)
    row = t // COLUMNS
    col = lax.rem(t, COLUMNS)
    north = (lax.rem(t + 128 - COLUMNS, 128), mp)
    south = (lax.rem(t + COLUMNS, 128), mp)
    east = (row * COLUMNS + lax.rem(col + 1, COLUMNS), mp)
    west = (row * COLUMNS + lax.rem(col + 7, COLUMNS), mp)
    other = (t + 1 - 2 * core, mp)

    y_par, m_par = lax.rem(y, 2), lax.rem(mp, 2)
    idx = z_hi * 2 + m_par
    p_to = jnp.where(y_par == 1, idx + 1, lax.rem(NY - idx, NY))
    y_to = lax.rem(2 * (y // 2) + p_to, NY)
    scatter_to = [(tile_of(x, y_to, hi, mp // 2), y // 2) for hi in range(2)]
    b_par, b_hi, b_ml = held_block(y, mp)
    scatter_from = [(tile_of(x, 2 * mp + b_par, b_hi, c), 2 * core + b_ml) for c in range(2)]

    def y_peer(d):
        return (tile_of(x, lax.rem(y + d, NY), z_hi, core), mp)

    def x_peer(e):
        return (tile_of(lax.rem(x + e, NX), y, z_hi, core), mp)

    greeted = [north, south, east, west] + scatter_to + scatter_from
    greeted += [y_peer(d) for d in range(1, NY)] + [x_peer(e) for e in range(1, NX)]
    for c in range(2):
        for d in range(4):
            if (c, d) != (0, 0):
                greeted.append((t - core + lax.rem(core + c, 2), lax.rem(mp + d, 4)))
    barrier = pltpu.get_barrier_semaphore()
    for device in greeted:
        pl.semaphore_signal(barrier, inc=1, device_id=device, device_id_type=MESH)

    for h in range(HEADS_DEV):
        lanes = slice(h * HD, (h + 1) * HD)
        for kv, ref in enumerate((k_ref, v_ref)):
            halves = to_halves(ref[:, lanes])
            for i in range(2):
                win[h, kv, 1 + i, STRIP : STRIP + 128, :] = halves[i]
    wpad[0:24, :] = w_ref[...]
    wpad[24:32, :] = jnp.zeros((8, HEADS_DEV * HD), jnp.bfloat16)
    gpair[core] = g_ref[...]
    pl.semaphore_wait(barrier, len(greeted))

    def remote(src, dst, send, recv, device):
        return pltpu.make_async_remote_copy(src, dst, send, recv, device_id=device, device_id_type=MESH)

    sent = []

    def send(src, dst, send_sem, recv_sem, device):
        copy = remote(src, dst, send_sem, recv_sem, device)
        copy.start()
        sent.append(copy)

    def wait_recv(dst, recv_sem):
        remote(dst, dst, recv_sem, recv_sem, other).wait_recv()

    for hi in range(2):
        device = scatter_to[hi]
        mine = (device[0] == t) & (device[1] == mp)
        copy = remote(wpad, stage.at[core], wsc_s.at[hi], wsc_r.at[core], device)
        here = pltpu.make_async_copy(wpad, stage.at[core], wsc_r.at[core])

        @pl.when(mine)
        def _():
            here.start()

        @pl.when(jnp.logical_not(mine))
        def _():
            copy.start()

    def top(h):
        return win.at[h, :, 1:3, STRIP : 2 * STRIP]

    def bottom(h):
        return win.at[h, :, 1:3, 2 * STRIP : 3 * STRIP]

    def halo_n(h):
        return win.at[h, :, 1:3, 0:STRIP]

    def halo_s(h):
        return win.at[h, :, 1:3, 3 * STRIP : 4 * STRIP]

    send(gpair.at[core], gpair.at[core], g_s, g_r, other)
    for h in range(HEADS_DEV):
        send(top(h), halo_s(h), kvns_s.at[h, 0], kvns_r.at[h, 0], north)
        send(bottom(h), halo_n(h), kvns_s.at[h, 1], kvns_r.at[h, 1], south)

    for c in range(2):
        wait_recv(stage.at[c], wsc_r.at[c])

    def block_at(x_at, y_at):
        par, hi, ml = held_block(y_at, mp)
        begin = pl.multiple_of(48 * ((par * 2 + hi) * NX + x_at), 16)
        return wbuf.at[ml, :, pl.ds(begin, 48), :]

    block = stage[:, 0:24, :].astype(jnp.float32).reshape(48, HEADS_DEV * HD).astype(jnp.bfloat16)
    begin = pl.multiple_of(48 * ((b_par * 2 + b_hi) * NX + x), 16)
    for h in range(HEADS_DEV):
        wbuf[b_ml, h, pl.ds(begin, 48), :] = block[:, h * HD : (h + 1) * HD]
    my_block = block_at(x, y)
    y_order = (1, 7, 2, 6, 3, 5, 4)
    x_order = (1, 3, 2)
    for i in range(7):
        d = y_order[i]
        send(my_block, my_block, wy_s.at[d], wy_r.at[d], y_peer(d))
    for e in x_order:
        send(my_block, my_block, wx_s.at[0, e], wx_r.at[0, e], x_peer(e))
    for d in y_order:
        theirs = block_at(x, lax.rem(y + NY - d, NY))
        wait_recv(theirs, wy_r.at[d])
        for e in x_order:
            send(theirs, theirs, wx_s.at[d, e], wx_r.at[d, e], x_peer(e))

    for h in range(HEADS_DEV):
        wait_recv(halo_s(h), kvns_r.at[h, 0])
        wait_recv(halo_n(h), kvns_r.at[h, 1])
        send(win.at[h, :, 1], win.at[h, :, 3], kvew_s.at[h, 0], kvew_r.at[h, 0], west)
        send(win.at[h, :, 2], win.at[h, :, 0], kvew_s.at[h, 1], kvew_r.at[h, 1], east)

    for d in (0,) + y_order:
        for e in x_order:
            theirs = block_at(lax.rem(x + NX - e, NX), lax.rem(y + NY - d, NY))
            wait_recv(theirs, wx_r.at[d, e])
    wait_recv(gpair.at[1 - core], g_r)

    def partial(h):
        weights = jnp.concatenate([wbuf[0, h], wbuf[1, h]], axis=1)
        for c in range(2):
            part[h, c] = jnp.dot(gpair[c], weights, preferred_element_type=jnp.float32).astype(jnp.bfloat16)

    def part_copies(h, ml, c):
        device = (t - core + c, 2 * core + ml)
        mine = (device[0] == t) & (device[1] == mp)
        src = part.at[h, c, :, ml * HD : (ml + 1) * HD]
        dst = arrived.at[h, mp]
        return (
            mine,
            pltpu.make_async_copy(src, dst, rs_r.at[h, mp]),
            remote(src, dst, rs_s.at[h, ml, c], rs_r.at[h, mp], device),
        )

    for h in range(HEADS_DEV):
        partial(h)
        for ml in range(2):
            for c in range(2):
                mine, here, copy = part_copies(h, ml, c)

                @pl.when(mine)
                def _():
                    here.start()

                @pl.when(jnp.logical_not(mine))
                def _():
                    copy.start()

    key_at = lax.broadcasted_iota(jnp.int32, (KEYS, CHUNK), 0)
    group = key_at // 256
    key_row = lax.rem(key_at, 256) // 8
    valid = (
        ((group > 0) | (col > 0))
        & ((group < 3) | (col < COLUMNS - 1))
        & ((key_row >= 8) | (row > 0))
        & ((key_row < 24) | (row < ROWS - 1))
    )
    bias[...] = jnp.where(valid, 0.0, -1e30)
    for h in range(HEADS_DEV):
        wait_recv(win.at[h, :, 3], kvew_r.at[h, 0])
        wait_recv(win.at[h, :, 0], kvew_r.at[h, 1])
        keys = win[h, 0].reshape(KEYS, HD)
        for i in range(2):
            rows = slice(i * CHUNK, (i + 1) * CHUNK)
            scores = lax.dot_general(
                keys, q_ref[rows, h * HD : (h + 1) * HD], LAST, preferred_element_type=jnp.float32
            )
            scores = scores * (SCALE * LOG2E) + bias[...]
            unnormed = jnp.exp2(scores - jnp.max(scores, axis=0, keepdims=True))
            prob[h, i] = unnormed * (1.0 / jnp.sum(unnormed, axis=0, keepdims=True))

    def spread_columns(h):
        send(ew_out.at[h, 0], ew_in.at[h, 0], dew_s.at[h, 0], dew_r.at[h, 0], west)
        send(ew_out.at[h, 1], ew_in.at[h, 1], dew_s.at[h, 1], dew_r.at[h, 1], east)

    def spread_rows(h):
        wait_recv(ew_in.at[h, 0], dew_r.at[h, 0])
        wait_recv(ew_in.at[h, 1], dew_r.at[h, 1])
        for kv in range(2):
            dwin[h, kv, 2] = dwin[h, kv, 2] + ew_in[h, 0, kv].astype(jnp.float32)
            dwin[h, kv, 1] = dwin[h, kv, 1] + ew_in[h, 1, kv].astype(jnp.float32)
            for i in range(2):
                ns_out[h, 0, kv, i] = dwin[h, kv, 1 + i, 0:STRIP].astype(jnp.bfloat16)
                ns_out[h, 1, kv, i] = dwin[h, kv, 1 + i, 3 * STRIP : 4 * STRIP].astype(jnp.bfloat16)
        send(ns_out.at[h, 0], ns_in.at[h, 0], dns_s.at[h, 0], dns_r.at[h, 0], north)
        send(ns_out.at[h, 1], ns_in.at[h, 1], dns_s.at[h, 1], dns_r.at[h, 1], south)

    for h in range(HEADS_DEV):
        lanes = slice(h * HD, (h + 1) * HD)
        total = jnp.zeros((TOK, HD), jnp.float32)
        for s in range(4):
            wait_recv(arrived.at[h, s], rs_r.at[h, s])
            total = total + arrived[h, s].astype(jnp.float32)
        cotangent = total.astype(jnp.bfloat16)
        keys = win[h, 0].reshape(KEYS, HD)
        values = win[h, 1].reshape(KEYS, HD)
        for i in range(2):
            rows = slice(i * CHUNK, (i + 1) * CHUNK)
            attention = prob[h, i]
            grad_attention = lax.dot_general(
                values, cotangent[rows], LAST, preferred_element_type=jnp.float32
            )
            row_total = jnp.sum(attention * grad_attention, axis=0, keepdims=True)
            grad_s[:, rows] = (attention * (grad_attention - row_total) * SCALE).astype(jnp.bfloat16)
            prob_low[:, rows] = attention.astype(jnp.bfloat16)
        dwin[h, 0] = jnp.dot(
            grad_s[...], q_ref[:, lanes], preferred_element_type=jnp.float32
        ).reshape(4, 256, HD)
        dwin[h, 1] = jnp.dot(
            prob_low[...], cotangent, preferred_element_type=jnp.float32
        ).reshape(4, 256, HD)
        for kv in range(2):
            ew_out[h, 0, kv] = dwin[h, kv, 0].astype(jnp.bfloat16)
            ew_out[h, 1, kv] = dwin[h, kv, 3].astype(jnp.bfloat16)
        spread_columns(h)
        dq_ref[:, lanes] = lax.dot_general(
            grad_s[...], keys, FIRST, preferred_element_type=jnp.float32
        ).astype(jnp.bfloat16)
        if h > 0:
            spread_rows(h - 1)
    spread_rows(HEADS_DEV - 1)

    for h in range(HEADS_DEV):
        lanes = slice(h * HD, (h + 1) * HD)
        wait_recv(ns_in.at[h, 0], dns_r.at[h, 0])
        wait_recv(ns_in.at[h, 1], dns_r.at[h, 1])
        for kv, ref in enumerate((dk_ref, dv_ref)):
            halves = []
            for i in range(2):
                upper = dwin[h, kv, 1 + i, STRIP : 2 * STRIP] + ns_in[h, 1, kv, i].astype(jnp.float32)
                lower = dwin[h, kv, 1 + i, 2 * STRIP : 3 * STRIP] + ns_in[h, 0, kv, i].astype(jnp.float32)
                halves.append(jnp.concatenate([upper, lower], axis=0).reshape(16, 8, HD))
            ref[:, lanes] = jnp.stack(halves, axis=1).reshape(TOK, HD).astype(jnp.bfloat16)

    for copy in sent:
        copy.wait_send()
    for hi in range(2):
        device = scatter_to[hi]
        mine = (device[0] == t) & (device[1] == mp)

        @pl.when(jnp.logical_not(mine))
        def _():
            remote(wpad, stage.at[core], wsc_s.at[hi], wsc_r.at[core], device).wait_send()

    for h in range(HEADS_DEV):
        for ml in range(2):
            for c in range(2):
                mine, here, copy = part_copies(h, ml, c)

                @pl.when(jnp.logical_not(mine))
                def _():
                    copy.wait_send()


def shards(query, key, value, grad_y, w_out):
    bf16, f32 = jnp.bfloat16, jnp.float32
    dma = pltpu.SemaphoreType.DMA
    out = jax.ShapeDtypeStruct(query.shape, bf16)
    vmem = pl.BlockSpec(memory_space=pltpu.VMEM)
    return pl.pallas_call(
        kernel,
        name="tiled_attention_backward",
        out_shape=(out, out, out),
        in_specs=[vmem] * 5,
        out_specs=(vmem,) * 3,
        scratch_shapes=[
            pltpu.VMEM((HEADS_DEV, 2, 4, 256, HD), bf16),
            pltpu.VMEM((32, HEADS_DEV * HD), bf16),
            pltpu.VMEM((2, 32, HEADS_DEV * HD), bf16),
            pltpu.VMEM((2, HEADS_DEV, K_DEV, HD), bf16),
            pltpu.VMEM((2, TOK, K_DEV), bf16),
            pltpu.VMEM((HEADS_DEV, 2, TOK, 2 * HD), bf16),
            pltpu.VMEM((HEADS_DEV, 4, TOK, HD), bf16),
            pltpu.VMEM((KEYS, CHUNK), f32),
            pltpu.VMEM((HEADS_DEV, 2, KEYS, CHUNK), f32),
            pltpu.VMEM((KEYS, TOK), bf16),
            pltpu.VMEM((KEYS, TOK), bf16),
            pltpu.VMEM((HEADS_DEV, 2, 4, 256, HD), f32),
            pltpu.VMEM((HEADS_DEV, 2, 2, 256, HD), bf16),
            pltpu.VMEM((HEADS_DEV, 2, 2, 256, HD), bf16),
            pltpu.VMEM((HEADS_DEV, 2, 2, 2, STRIP, HD), bf16),
            pltpu.VMEM((HEADS_DEV, 2, 2, 2, STRIP, HD), bf16),
            dma((HEADS_DEV, 2)), dma((HEADS_DEV, 2)),
            dma((HEADS_DEV, 2)), dma((HEADS_DEV, 2)),
            dma((2,)), dma((2,)),
            dma, dma,
            dma((NY,)), dma((NY,)),
            dma((NY, NX)), dma((NY, NX)),
            dma((HEADS_DEV, 2, 2)), dma((HEADS_DEV, 4)),
            dma((HEADS_DEV, 2)), dma((HEADS_DEV, 2)),
            dma((HEADS_DEV, 2)), dma((HEADS_DEV, 2)),
        ],
        compiler_params=pltpu.CompilerParams(
            collective_id=0, has_side_effects=True, vmem_limit_bytes=48 * 1024 * 1024
        ),
    )(query, key, value, grad_y, w_out)


def solution(mesh):
    spec = P("tile", "mp")
    return jax.shard_map(
        shards, mesh=mesh, in_specs=(spec,) * 5, out_specs=(spec,) * 3, check_vma=False
    )
```

time: 301 us -> 100 us (0.33)
  the two profiles are of different devices: /device:TPU:57 before, /device:TPU:217 now
where the time goes in v1:
time: 100 us
  Pallas kernels  92.9 us (93%)
  local copies, waits for them, and re-layouts  6.52 us (7%)
    pallas_call x1, Pallas kernels, shards(): pl.pallas_call(kernel, name='tiled_attention_backward', out_shape=(out, o...  92.9 us
    unnamed x13, local copies, waits for them, and re-layouts  6.52 us

profile of v1, /device:TPU:217, one launch (start us, length us, event | category | flops | bytes accessed | tf_op | source)
XLA Modules:
  0.0 100.1 jit_solution(4198641724108527575)
XLA Ops:
  0.6 0.0 copy-start
  0.6 1.0 copy-done
  1.6 0.0 copy-start.1
  1.6 0.9 copy-done.1
  2.6 0.0 copy-start.2
  2.6 0.9 copy-done.2
  3.5 0.0 copy-start.3
  3.5 0.9 copy-done.3
  4.4 0.0 copy-start.4
  4.4 0.7 copy-done.4
  5.1 92.9 %tiled_attention_backward.1 = (bf16[256,384]{1,0:T(8,128)(2,1)S(1)}, bf16[256,384]{1,0:T(8,128)(2,1)S(1)}, bf16[256,384]{1,0:T(8,128)(2,1)S(1)}) custom-call(bf16[256,384]{1,0:T(8,128)(2,1)S(1)} %copy-done.1, bf16[256,384]{1,0:T(8,128)(2,1)S(1)} %copy-done.2, bf16[256,384]{1,0:T(8,128)(2,1)S(1)} %copy-done.3, bf16[256,768]{1,0:T(8,128)(2,1)S(1)} %copy-done, ...), custom_call_target="tpu_custom_call" | custom-call | tf_op jit(solution)/shard_map/tiled_attention_backward/pallas_call | solution.py:322
  98.0 0.7 copy.11
  98.7 0.7 copy.12
  99.4 0.7 copy.13
Async XLA Ops:
  0.6 1.0 copy-start
  1.6 0.9 copy-start.1
  2.6 0.9 copy-start.2
  3.5 0.9 copy-start.3
  4.4 0.7 copy-start.4

commit v2 on v1

--- a/solution.py
+++ b/solution.py
@@ -16,6 +16,7 @@
 KEYS = 1024
 CHUNK = 128
 K_DEV = 768
+K_PAIR = 1536
 LOG2E = 1.4426950408889634
 SCALE = HD ** (-0.5)
 MESH = pl.DeviceIdType.MESH
@@ -28,11 +29,8 @@
 
 
 def held_block(y, mp):
-    p = lax.rem(y - 2 * mp + 2 * NY, NY)
-    upper = (p >= 1) & (p <= 4)
-    parity = jnp.where(upper, 1, 0)
-    idx = jnp.where(upper, p - 1, lax.rem(NY - p, NY))
-    return parity, idx // 2, lax.rem(idx, 2)
+    p = lax.rem(y - 4 * (mp // 2) + NY, NY)
+    return jnp.where(p < 4, p, 7 - p), jnp.where(p < 4, 0, 1)
 
 
 def to_halves(tokens):
@@ -41,11 +39,11 @@
 
 
 def kernel(
-    q_ref, k_ref, v_ref, g_ref, w_ref, dq_ref, dk_ref, dv_ref,
-    win, wpad, stage, wbuf, gpair, part, arrived, bias, prob, grad_s, prob_low, dwin,
-    ew_out, ew_in, ns_out, ns_in,
+    q_hbm, k_hbm, v_hbm, g_hbm, w_hbm, dq_ref, dk_ref, dv_ref,
+    win, wpad, stage, wbuf, gall, part, arrived, bias, prob, grad_s, prob_low, dwin,
+    ew_out, ew_in, ns_out, ns_in, q, k, v, w,
     kvns_s, kvns_r, kvew_s, kvew_r, wsc_s, wsc_r, g_s, g_r, wy_s, wy_r, wx_s, wx_r,
-    rs_s, rs_r, dew_s, dew_r, dns_s, dns_r,
+    rs_s, rs_r, dew_s, dew_r, dns_s, dns_r, load,
 ):
     t = lax.axis_index("tile")
     mp = lax.axis_index("mp")
@@ -61,13 +59,17 @@
     west = (row * COLUMNS + lax.rem(col + 7, COLUMNS), mp)
     other = (t + 1 - 2 * core, mp)
 
-    y_par, m_par = lax.rem(y, 2), lax.rem(mp, 2)
-    idx = z_hi * 2 + m_par
-    p_to = jnp.where(y_par == 1, idx + 1, lax.rem(NY - idx, NY))
-    y_to = lax.rem(2 * (y // 2) + p_to, NY)
-    scatter_to = [(tile_of(x, y_to, hi, mp // 2), y // 2) for hi in range(2)]
-    b_par, b_hi, b_ml = held_block(y, mp)
-    scatter_from = [(tile_of(x, 2 * mp + b_par, b_hi, c), 2 * core + b_ml) for c in range(2)]
+    half, within = y // 4, lax.rem(y, 4)
+    y_to = jnp.where(z_hi == 0, y, lax.rem(4 * half + 7 - within, NY))
+    scatter_to = [(tile_of(x, y_to, hi, mp // 2), 2 * half + lax.rem(mp, 2)) for hi in range(2)]
+    b_in, b_hi = held_block(y, mp)
+    scatter_from = [
+        (tile_of(x, 4 * (mp // 2) + b_in, b_hi, c), lax.rem(mp, 2) + 2 * core) for c in range(2)
+    ]
+    side = lax.rem(mp, 2)
+    pair = mp + 1 - 2 * side
+    far = lax.rem(mp + 2, 4)
+    block_of_heads = side + 2 * core
 
     def y_peer(d):
         return (tile_of(x, lax.rem(y + d, NY), z_hi, core), mp)
@@ -77,23 +79,30 @@
 
     greeted = [north, south, east, west] + scatter_to + scatter_from
     greeted += [y_peer(d) for d in range(1, NY)] + [x_peer(e) for e in range(1, NX)]
-    for c in range(2):
-        for d in range(4):
-            if (c, d) != (0, 0):
-                greeted.append((t - core + lax.rem(core + c, 2), lax.rem(mp + d, 4)))
+    greeted += [(t, pair), (t, far), (other[0], far)]
     barrier = pltpu.get_barrier_semaphore()
     for device in greeted:
         pl.semaphore_signal(barrier, inc=1, device_id=device, device_id_type=MESH)
 
+    loads = []
+    for i, (src, dst) in enumerate(
+        ((w_hbm, w), (k_hbm, k), (v_hbm, v), (g_hbm, gall.at[side, core]), (q_hbm, q))
+    ):
+        loads.append(pltpu.make_async_copy(src, dst, load.at[i]))
+        loads[-1].start()
+
+    loads[0].wait()
+    wpad[0:24, :] = w[...]
+    wpad[24:32, :] = jnp.zeros((8, HEADS_DEV * HD), jnp.bfloat16)
+    loads[1].wait()
+    loads[2].wait()
     for h in range(HEADS_DEV):
         lanes = slice(h * HD, (h + 1) * HD)
-        for kv, ref in enumerate((k_ref, v_ref)):
+        for kv, ref in enumerate((k, v)):
             halves = to_halves(ref[:, lanes])
             for i in range(2):
                 win[h, kv, 1 + i, STRIP : STRIP + 128, :] = halves[i]
-    wpad[0:24, :] = w_ref[...]
-    wpad[24:32, :] = jnp.zeros((8, HEADS_DEV * HD), jnp.bfloat16)
-    gpair[core] = g_ref[...]
+    loads[3].wait()
     pl.semaphore_wait(barrier, len(greeted))
 
     def remote(src, dst, send, recv, device):
@@ -112,16 +121,14 @@
     for hi in range(2):
         device = scatter_to[hi]
         mine = (device[0] == t) & (device[1] == mp)
-        copy = remote(wpad, stage.at[core], wsc_s.at[hi], wsc_r.at[core], device)
-        here = pltpu.make_async_copy(wpad, stage.at[core], wsc_r.at[core])
 
         @pl.when(mine)
         def _():
-            here.start()
+            pltpu.make_async_copy(wpad, stage.at[core], wsc_r.at[core]).start()
 
         @pl.when(jnp.logical_not(mine))
         def _():
-            copy.start()
+            remote(wpad, stage.at[core], wsc_s.at[hi], wsc_r.at[core], device).start()
 
     def top(h):
         return win.at[h, :, 1:3, STRIP : 2 * STRIP]
@@ -135,7 +142,10 @@
     def halo_s(h):
         return win.at[h, :, 1:3, 3 * STRIP : 4 * STRIP]
 
-    send(gpair.at[core], gpair.at[core], g_s, g_r, other)
+    mine_g = gall.at[side, core]
+    near_g = gall.at[1 - side, core]
+    send(mine_g, mine_g, g_s.at[0], g_r.at[0], (t, pair))
+    send(mine_g, mine_g, g_s.at[1], g_r.at[1], other)
     for h in range(HEADS_DEV):
         send(top(h), halo_s(h), kvns_s.at[h, 0], kvns_r.at[h, 0], north)
         send(bottom(h), halo_n(h), kvns_s.at[h, 1], kvns_r.at[h, 1], south)
@@ -144,19 +154,18 @@
         wait_recv(stage.at[c], wsc_r.at[c])
 
     def block_at(x_at, y_at):
-        par, hi, ml = held_block(y_at, mp)
-        begin = pl.multiple_of(48 * ((par * 2 + hi) * NX + x_at), 16)
-        return wbuf.at[ml, :, pl.ds(begin, 48), :]
+        inside, hi = held_block(y_at, mp)
+        begin = pl.multiple_of(48 * ((inside * 2 + hi) * NX + x_at), 16)
+        return wbuf.at[:, pl.ds(begin, 48), :]
 
     block = stage[:, 0:24, :].astype(jnp.float32).reshape(48, HEADS_DEV * HD).astype(jnp.bfloat16)
-    begin = pl.multiple_of(48 * ((b_par * 2 + b_hi) * NX + x), 16)
-    for h in range(HEADS_DEV):
-        wbuf[b_ml, h, pl.ds(begin, 48), :] = block[:, h * HD : (h + 1) * HD]
+    begin = pl.multiple_of(48 * ((b_in * 2 + b_hi) * NX + x), 16)
+    for h in range(HEADS_DEV):
+        wbuf[h, pl.ds(begin, 48), :] = block[:, h * HD : (h + 1) * HD]
     my_block = block_at(x, y)
     y_order = (1, 7, 2, 6, 3, 5, 4)
     x_order = (1, 3, 2)
-    for i in range(7):
-        d = y_order[i]
+    for d in y_order:
         send(my_block, my_block, wy_s.at[d], wy_r.at[d], y_peer(d))
     for e in x_order:
         send(my_block, my_block, wx_s.at[0, e], wx_r.at[0, e], x_peer(e))
@@ -166,48 +175,50 @@
         for e in x_order:
             send(theirs, theirs, wx_s.at[d, e], wx_r.at[d, e], x_peer(e))
 
+    wait_recv(near_g, g_r.at[0])
+    send(near_g, near_g, g_s.at[2], g_r.at[2], other)
+    wait_recv(gall.at[side, 1 - core], g_r.at[1])
+    wait_recv(gall.at[1 - side, 1 - core], g_r.at[2])
+
+    for d in (0,) + y_order:
+        for e in x_order:
+            theirs = block_at(lax.rem(x + NX - e, NX), lax.rem(y + NY - d, NY))
+            wait_recv(theirs, wx_r.at[d, e])
+
+    slot = jnp.where(block_of_heads == mp, 0, 1)
+
+    def part_copy(h, c):
+        device = (t - core + c, block_of_heads)
+        mine = (block_of_heads == mp) & (core == c)
+        return mine, remote(part.at[h, c], arrived.at[h, slot], rs_s.at[h, c], rs_r.at[h, slot], device)
+
+    for h in range(HEADS_DEV):
+        total = jnp.zeros((2 * TOK, HD), jnp.float32)
+        for i in range(2):
+            total = total + jnp.dot(
+                gall[i].reshape(2 * TOK, K_DEV),
+                wbuf[h, i * K_DEV : (i + 1) * K_DEV, :],
+                preferred_element_type=jnp.float32,
+            )
+        part[h] = total.reshape(2, TOK, HD).astype(jnp.bfloat16)
+        for c in range(2):
+            mine, copy = part_copy(h, c)
+
+            @pl.when(mine)
+            def _():
+                pltpu.make_async_copy(part.at[h, c], arrived.at[h, slot], rs_r.at[h, slot]).start()
+
+            @pl.when(jnp.logical_not(mine))
+            def _():
+                copy.start()
+
     for h in range(HEADS_DEV):
         wait_recv(halo_s(h), kvns_r.at[h, 0])
         wait_recv(halo_n(h), kvns_r.at[h, 1])
         send(win.at[h, :, 1], win.at[h, :, 3], kvew_s.at[h, 0], kvew_r.at[h, 0], west)
         send(win.at[h, :, 2], win.at[h, :, 0], kvew_s.at[h, 1], kvew_r.at[h, 1], east)
 
-    for d in (0,) + y_order:
-        for e in x_order:
-            theirs = block_at(lax.rem(x + NX - e, NX), lax.rem(y + NY - d, NY))
-            wait_recv(theirs, wx_r.at[d, e])
-    wait_recv(gpair.at[1 - core], g_r)
-
-    def partial(h):
-        weights = jnp.concatenate([wbuf[0, h], wbuf[1, h]], axis=1)
-        for c in range(2):
-            part[h, c] = jnp.dot(gpair[c], weights, preferred_element_type=jnp.float32).astype(jnp.bfloat16)
-
-    def part_copies(h, ml, c):
-        device = (t - core + c, 2 * core + ml)
-        mine = (device[0] == t) & (device[1] == mp)
-        src = part.at[h, c, :, ml * HD : (ml + 1) * HD]
-        dst = arrived.at[h, mp]
-        return (
-            mine,
-            pltpu.make_async_copy(src, dst, rs_r.at[h, mp]),
-            remote(src, dst, rs_s.at[h, ml, c], rs_r.at[h, mp], device),
-        )
-
-    for h in range(HEADS_DEV):
-        partial(h)
-        for ml in range(2):
-            for c in range(2):
-                mine, here, copy = part_copies(h, ml, c)
-
-                @pl.when(mine)
-                def _():
-                    here.start()
-
-                @pl.when(jnp.logical_not(mine))
-                def _():
-                    copy.start()
-
+    loads[4].wait()
     key_at = lax.broadcasted_iota(jnp.int32, (KEYS, CHUNK), 0)
     group = key_at // 256
     key_row = lax.rem(key_at, 256) // 8
@@ -225,7 +236,7 @@
         for i in range(2):
             rows = slice(i * CHUNK, (i + 1) * CHUNK)
             scores = lax.dot_general(
-                keys, q_ref[rows, h * HD : (h + 1) * HD], LAST, preferred_element_type=jnp.float32
+                keys, q[rows, h * HD : (h + 1) * HD], LAST, preferred_element_type=jnp.float32
             )
             scores = scores * (SCALE * LOG2E) + bias[...]
             unnormed = jnp.exp2(scores - jnp.max(scores, axis=0, keepdims=True))
@@ -250,7 +261,7 @@
     for h in range(HEADS_DEV):
         lanes = slice(h * HD, (h + 1) * HD)
         total = jnp.zeros((TOK, HD), jnp.float32)
-        for s in range(4):
+        for s in range(2):
             wait_recv(arrived.at[h, s], rs_r.at[h, s])
             total = total + arrived[h, s].astype(jnp.float32)
         cotangent = total.astype(jnp.bfloat16)
@@ -266,7 +277,7 @@
             grad_s[:, rows] = (attention * (grad_attention - row_total) * SCALE).astype(jnp.bfloat16)
             prob_low[:, rows] = attention.astype(jnp.bfloat16)
         dwin[h, 0] = jnp.dot(
-            grad_s[...], q_ref[:, lanes], preferred_element_type=jnp.float32
+            grad_s[...], q[:, lanes], preferred_element_type=jnp.float32
         ).reshape(4, 256, HD)
         dwin[h, 1] = jnp.dot(
             prob_low[...], cotangent, preferred_element_type=jnp.float32
@@ -305,13 +316,12 @@
             remote(wpad, stage.at[core], wsc_s.at[hi], wsc_r.at[core], device).wait_send()
 
     for h in range(HEADS_DEV):
-        for ml in range(2):
-            for c in range(2):
-                mine, here, copy = part_copies(h, ml, c)
-
-                @pl.when(jnp.logical_not(mine))
-                def _():
-                    copy.wait_send()
+        for c in range(2):
+            mine, copy = part_copy(h, c)
+
+            @pl.when(jnp.logical_not(mine))
+            def _():
+                copy.wait_send()
 
 
 def shards(query, key, value, grad_y, w_out):
@@ -319,20 +329,21 @@
     dma = pltpu.SemaphoreType.DMA
     out = jax.ShapeDtypeStruct(query.shape, bf16)
     vmem = pl.BlockSpec(memory_space=pltpu.VMEM)
+    hbm = pl.BlockSpec(memory_space=pltpu.HBM)
     return pl.pallas_call(
         kernel,
         name="tiled_attention_backward",
         out_shape=(out, out, out),
-        in_specs=[vmem] * 5,
+        in_specs=[hbm] * 5,
         out_specs=(vmem,) * 3,
         scratch_shapes=[
             pltpu.VMEM((HEADS_DEV, 2, 4, 256, HD), bf16),
             pltpu.VMEM((32, HEADS_DEV * HD), bf16),
             pltpu.VMEM((2, 32, HEADS_DEV * HD), bf16),
-            pltpu.VMEM((2, HEADS_DEV, K_DEV, HD), bf16),
-            pltpu.VMEM((2, TOK, K_DEV), bf16),
-            pltpu.VMEM((HEADS_DEV, 2, TOK, 2 * HD), bf16),
-            pltpu.VMEM((HEADS_DEV, 4, TOK, HD), bf16),
+            pltpu.VMEM((HEADS_DEV, K_PAIR, HD), bf16),
+            pltpu.VMEM((2, 2, TOK, K_DEV), bf16),
+            pltpu.VMEM((HEADS_DEV, 2, TOK, HD), bf16),
+            pltpu.VMEM((HEADS_DEV, 2, TOK, HD), bf16),
             pltpu.VMEM((KEYS, CHUNK), f32),
             pltpu.VMEM((HEADS_DEV, 2, KEYS, CHUNK), f32),
             pltpu.VMEM((KEYS, TOK), bf16),
@@ -342,15 +353,20 @@
             pltpu.VMEM((HEADS_DEV, 2, 2, 256, HD), bf16),
             pltpu.VMEM((HEADS_DEV, 2, 2, 2, STRIP, HD), bf16),
             pltpu.VMEM((HEADS_DEV, 2, 2, 2, STRIP, HD), bf16),
+            pltpu.VMEM(query.shape, bf16),
+            pltpu.VMEM(key.shape, bf16),
+            pltpu.VMEM(value.shape, bf16),
+            pltpu.VMEM(w_out.shape, bf16),
             dma((HEADS_DEV, 2)), dma((HEADS_DEV, 2)),
             dma((HEADS_DEV, 2)), dma((HEADS_DEV, 2)),
             dma((2,)), dma((2,)),
-            dma, dma,
+            dma((3,)), dma((3,)),
             dma((NY,)), dma((NY,)),
             dma((NY, NX)), dma((NY, NX)),
-            dma((HEADS_DEV, 2, 2)), dma((HEADS_DEV, 4)),
-            dma((HEADS_DEV, 2)), dma((HEADS_DEV, 2)),
-            dma((HEADS_DEV, 2)), dma((HEADS_DEV, 2)),
+            dma((HEADS_DEV, 2)), dma((HEADS_DEV, 2)),
+            dma((HEADS_DEV, 2)), dma((HEADS_DEV, 2)),
+            dma((HEADS_DEV, 2)), dma((HEADS_DEV, 2)),
+            dma((5,)),
         ],
         compiler_params=pltpu.CompilerParams(
             collective_id=0, has_side_effects=True, vmem_limit_bytes=48 * 1024 * 1024

time: 100 us -> 86.2 us (0.86)
  the two profiles are of different devices: /device:TPU:217 before, /device:TPU:1 now
where the time goes in v2:
time: 86.2 us; the launch traced here: 85.9 us
  Pallas kernels  78.8 us (91%)
  local copies, waits for them, and re-layouts  6.52 us (8%)
    pallas_call x1, Pallas kernels, shards(): pl.pallas_call(kernel, name='tiled_attention_backward', out_shape=(out, o...  78.8 us
    unnamed x13, local copies, waits for them, and re-layouts  6.52 us

profile of v2, /device:TPU:1, one launch (start us, length us, event | category | flops | bytes accessed | tf_op | source)
XLA Modules:
  0.0 85.9 jit_solution(14380348238807314073)
XLA Ops:
  0.6 0.0 copy-start
  0.6 1.0 %copy-done = bf16[256,768]{1,0:T(8,128)(2,1)S(1)} copy-done((bf16[256,768]{1,0:T(8,128)(2,1)S(1)}, bf16[256,768]{1,0:T(8,128)(2,1)}, u32[]{:S(2)}) %copy-start) | copy-done | bytes 393240
  1.6 0.0 copy-start.1
  1.6 0.9 %copy-done.1 = bf16[256,384]{1,0:T(8,128)(2,1)S(1)} copy-done((bf16[256,384]{1,0:T(8,128)(2,1)S(1)}, bf16[256,384]{1,0:T(8,128)(2,1)}, u32[]{:S(2)}) %copy-start.1) | copy-done | bytes 196632
  2.6 0.0 copy-start.2
  2.6 0.9 %copy-done.2 = bf16[256,384]{1,0:T(8,128)(2,1)S(1)} copy-done((bf16[256,384]{1,0:T(8,128)(2,1)S(1)}, bf16[256,384]{1,0:T(8,128)(2,1)}, u32[]{:S(2)}) %copy-start.2) | copy-done | bytes 196632
  3.5 0.0 copy-start.3
  3.5 0.9 %copy-done.3 = bf16[256,384]{1,0:T(8,128)(2,1)S(1)} copy-done((bf16[256,384]{1,0:T(8,128)(2,1)S(1)}, bf16[256,384]{1,0:T(8,128)(2,1)}, u32[]{:S(2)}) %copy-start.3) | copy-done | bytes 196632
  4.4 0.0 copy-start.4
  4.4 0.7 copy-done.4
  5.1 78.8 %tiled_attention_backward.1 = (bf16[256,384]{1,0:T(8,128)(2,1)S(1)}, bf16[256,384]{1,0:T(8,128)(2,1)S(1)}, bf16[256,384]{1,0:T(8,128)(2,1)S(1)}) custom-call(bf16[256,384]{1,0:T(8,128)(2,1)S(1)} %copy-done.1, bf16[256,384]{1,0:T(8,128)(2,1)S(1)} %copy-done.2, bf16[256,384]{1,0:T(8,128)(2,1)S(1)} %copy-done.3, bf16[256,768]{1,0:T(8,128)(2,1)S(1)} %copy-done, ...), custom_call_target="tpu_custom_call" | custom-call | tf_op jit(solution)/shard_map/tiled_attention_backward/pallas_call | solution.py:333
  83.9 0.7 copy.11
  84.6 0.7 copy.12
  85.3 0.7 copy.13
Async XLA Ops:
  0.6 1.0 %copy-start = (bf16[256,768]{1,0:T(8,128)(2,1)S(1)}, bf16[256,768]{1,0:T(8,128)(2,1)}, u32[]{:S(2)}) copy-start(bf16[256,768]{1,0:T(8,128)(2,1)} %g_hbm.1) | copy-start | bytes 1179652
  1.6 0.9 %copy-start.1 = (bf16[256,384]{1,0:T(8,128)(2,1)S(1)}, bf16[256,384]{1,0:T(8,128)(2,1)}, u32[]{:S(2)}) copy-start(bf16[256,384]{1,0:T(8,128)(2,1)} %q_hbm.1) | copy-start | bytes 589828
  2.6 0.9 %copy-start.2 = (bf16[256,384]{1,0:T(8,128)(2,1)S(1)}, bf16[256,384]{1,0:T(8,128)(2,1)}, u32[]{:S(2)}) copy-start(bf16[256,384]{1,0:T(8,128)(2,1)} %k_hbm.1) | copy-start | bytes 589828
  3.5 0.9 %copy-start.3 = (bf16[256,384]{1,0:T(8,128)(2,1)S(1)}, bf16[256,384]{1,0:T(8,128)(2,1)}, u32[]{:S(2)}) copy-start(bf16[256,384]{1,0:T(8,128)(2,1)} %v_hbm.1) | copy-start | bytes 589828
  4.4 0.7 copy-start.4

commit v3 on v2

--- a/solution.py
+++ b/solution.py
@@ -146,9 +146,20 @@
     near_g = gall.at[1 - side, core]
     send(mine_g, mine_g, g_s.at[0], g_r.at[0], (t, pair))
     send(mine_g, mine_g, g_s.at[1], g_r.at[1], other)
-    for h in range(HEADS_DEV):
+
+    def halo_rows(h):
         send(top(h), halo_s(h), kvns_s.at[h, 0], kvns_r.at[h, 0], north)
         send(bottom(h), halo_n(h), kvns_s.at[h, 1], kvns_r.at[h, 1], south)
+
+    def halo_columns(h):
+        wait_recv(halo_s(h), kvns_r.at[h, 0])
+        wait_recv(halo_n(h), kvns_r.at[h, 1])
+        send(win.at[h, :, 1], win.at[h, :, 3], kvew_s.at[h, 0], kvew_r.at[h, 0], west)
+        send(win.at[h, :, 2], win.at[h, :, 0], kvew_s.at[h, 1], kvew_r.at[h, 1], east)
+
+    halo_rows(0)
+    halo_rows(1)
+    halo_rows(2)
 
     for c in range(2):
         wait_recv(stage.at[c], wsc_r.at[c])
@@ -192,7 +203,7 @@
         mine = (block_of_heads == mp) & (core == c)
         return mine, remote(part.at[h, c], arrived.at[h, slot], rs_s.at[h, c], rs_r.at[h, slot], device)
 
-    for h in range(HEADS_DEV):
+    def share(h):
         total = jnp.zeros((2 * TOK, HD), jnp.float32)
         for i in range(2):
             total = total + jnp.dot(
@@ -212,12 +223,13 @@
             def _():
                 copy.start()
 
-    for h in range(HEADS_DEV):
-        wait_recv(halo_s(h), kvns_r.at[h, 0])
-        wait_recv(halo_n(h), kvns_r.at[h, 1])
-        send(win.at[h, :, 1], win.at[h, :, 3], kvew_s.at[h, 0], kvew_r.at[h, 0], west)
-        send(win.at[h, :, 2], win.at[h, :, 0], kvew_s.at[h, 1], kvew_r.at[h, 1], east)
-
+    share(0)
+    share(1)
+    share(2)
+
+    halo_columns(0)
+    halo_columns(1)
+    halo_columns(2)
     loads[4].wait()
     key_at = lax.broadcasted_iota(jnp.int32, (KEYS, CHUNK), 0)
     group = key_at // 256
@@ -229,7 +241,8 @@
         & ((key_row < 24) | (row < ROWS - 1))
     )
     bias[...] = jnp.where(valid, 0.0, -1e30)
-    for h in range(HEADS_DEV):
+
+    def softmax(h):
         wait_recv(win.at[h, :, 3], kvew_r.at[h, 0])
         wait_recv(win.at[h, :, 0], kvew_r.at[h, 1])
         keys = win[h, 0].reshape(KEYS, HD)
@@ -258,7 +271,7 @@
         send(ns_out.at[h, 0], ns_in.at[h, 0], dns_s.at[h, 0], dns_r.at[h, 0], north)
         send(ns_out.at[h, 1], ns_in.at[h, 1], dns_s.at[h, 1], dns_r.at[h, 1], south)
 
-    for h in range(HEADS_DEV):
+    def backward(h):
         lanes = slice(h * HD, (h + 1) * HD)
         total = jnp.zeros((TOK, HD), jnp.float32)
         for s in range(2):
@@ -289,11 +302,8 @@
         dq_ref[:, lanes] = lax.dot_general(
             grad_s[...], keys, FIRST, preferred_element_type=jnp.float32
         ).astype(jnp.bfloat16)
-        if h > 0:
-            spread_rows(h - 1)
-    spread_rows(HEADS_DEV - 1)
-
-    for h in range(HEADS_DEV):
+
+    def finish(h):
         lanes = slice(h * HD, (h + 1) * HD)
         wait_recv(ns_in.at[h, 0], dns_r.at[h, 0])
         wait_recv(ns_in.at[h, 1], dns_r.at[h, 1])
@@ -304,6 +314,18 @@
                 lower = dwin[h, kv, 1 + i, 2 * STRIP : 3 * STRIP] + ns_in[h, 0, kv, i].astype(jnp.float32)
                 halves.append(jnp.concatenate([upper, lower], axis=0).reshape(16, 8, HD))
             ref[:, lanes] = jnp.stack(halves, axis=1).reshape(TOK, HD).astype(jnp.bfloat16)
+
+    softmax(0)
+    backward(0)
+    softmax(1)
+    spread_rows(0)
+    backward(1)
+    softmax(2)
+    spread_rows(1)
+    backward(2)
+    spread_rows(2)
+    for h in range(HEADS_DEV):
+        finish(h)
 
     for copy in sent:
         copy.wait_send()
@@ -369,7 +391,7 @@
             dma((5,)),
         ],
         compiler_params=pltpu.CompilerParams(
-            collective_id=0, has_side_effects=True, vmem_limit_bytes=48 * 1024 * 1024
+            collective_id=0, has_side_effects=True, vmem_limit_bytes=60 * 1024 * 1024
         ),
     )(query, key, value, grad_y, w_out)
 

time: 86.2 us -> 81.1 us (0.941)
  the two profiles are of different devices: /device:TPU:1 before, /device:TPU:57 now
where the time goes in v3:
time: 81.1 us; the launch traced here: 80 us
  Pallas kernels  76 us (94%)
  local copies, waits for them, and re-layouts  3.34 us (4%)
    pallas_call x1, Pallas kernels, shards(): pl.pallas_call(kernel, name='tiled_attention_backward', out_shape=(out, o...  76 us
    unnamed x7, local copies, waits for them, and re-layouts  3.34 us

profile of v3, /device:TPU:57, one launch (start us, length us, event | category | flops | bytes accessed | tf_op | source)
XLA Modules:
  0.0 80.0 jit_solution(10737307636844671975)
XLA Ops:
  0.6 76.0 %tiled_attention_backward.1 = (bf16[256,384]{1,0:T(8,128)(2,1)}, bf16[256,384]{1,0:T(8,128)(2,1)}, bf16[256,384]{1,0:T(8,128)(2,1)}) custom-call(bf16[256,384]{1,0:T(8,128)(2,1)} %q_hbm.1, bf16[256,384]{1,0:T(8,128)(2,1)} %k_hbm.1, bf16[256,384]{1,0:T(8,128)(2,1)} %v_hbm.1, bf16[256,768]{1,0:T(8,128)(2,1)} %g_hbm.1, bf16[24,384]{1,0:T(8,128)(2,1)} %w_hbm.1), custom_call_target="tpu_custom_call" | custom-call | tf_op jit(solution)/shard_map/tiled_attention_backward/pallas_call | solution.py:355
  76.6 0.0 copy-start.1
  76.6 1.7 %copy.11 = bf16[256,384]{1,0:T(8,128)(2,1)} copy(bf16[256,384]{1,0:T(8,128)(2,1)} %get-tuple-element.6) | data formatting | bytes 393216
  78.3 0.0 copy-done.1
  78.3 0.0 copy-start
  78.3 0.7 copy.12
  79.0 0.3 copy-done
  79.3 0.7 copy.13
Async XLA Ops:
  76.6 1.7 %copy-start.1 = (bf16[256,384]{1,0:T(8,128)(2,1)S(1)}, bf16[256,384]{1,0:T(8,128)(2,1)}, u32[]{:S(2)}) copy-start(bf16[256,384]{1,0:T(8,128)(2,1)} %get-tuple-element.7) | copy-start | bytes 589828
  78.3 1.0 %copy-start = (bf16[256,384]{1,0:T(8,128)(2,1)S(1)}, bf16[256,384]{1,0:T(8,128)(2,1)}, u32[]{:S(2)}) copy-start(bf16[256,384]{1,0:T(8,128)(2,1)} %get-tuple-element.8) | copy-start | bytes 589828

commit v4 on v3

--- a/solution.py
+++ b/solution.py
@@ -39,11 +39,11 @@
 
 
 def kernel(
-    q_hbm, k_hbm, v_hbm, g_hbm, w_hbm, dq_ref, dk_ref, dv_ref,
+    q_hbm, k_hbm, v_hbm, g_hbm, w_hbm, dq_hbm, dk_hbm, dv_hbm,
     win, wpad, stage, wbuf, gall, part, arrived, bias, prob, grad_s, prob_low, dwin,
-    ew_out, ew_in, ns_out, ns_in, q, k, v, w,
+    ew_out, ew_in, ns_out, ns_in, q, k, v, w, out,
     kvns_s, kvns_r, kvew_s, kvew_r, wsc_s, wsc_r, g_s, g_r, wy_s, wy_r, wx_s, wx_r,
-    rs_s, rs_r, dew_s, dew_r, dns_s, dns_r, load,
+    rs_s, rs_r, dew_s, dew_r, dns_s, dns_r, load, store,
 ):
     t = lax.axis_index("tile")
     mp = lax.axis_index("mp")
@@ -159,7 +159,6 @@
 
     halo_rows(0)
     halo_rows(1)
-    halo_rows(2)
 
     for c in range(2):
         wait_recv(stage.at[c], wsc_r.at[c])
@@ -185,6 +184,7 @@
         wait_recv(theirs, wy_r.at[d])
         for e in x_order:
             send(theirs, theirs, wx_s.at[d, e], wx_r.at[d, e], x_peer(e))
+    halo_rows(2)
 
     wait_recv(near_g, g_r.at[0])
     send(near_g, near_g, g_s.at[2], g_r.at[2], other)
@@ -228,8 +228,6 @@
     share(2)
 
     halo_columns(0)
-    halo_columns(1)
-    halo_columns(2)
     loads[4].wait()
     key_at = lax.broadcasted_iota(jnp.int32, (KEYS, CHUNK), 0)
     group = key_at // 256
@@ -254,6 +252,13 @@
             scores = scores * (SCALE * LOG2E) + bias[...]
             unnormed = jnp.exp2(scores - jnp.max(scores, axis=0, keepdims=True))
             prob[h, i] = unnormed * (1.0 / jnp.sum(unnormed, axis=0, keepdims=True))
+
+    stores = []
+
+    def leave(i, ref, h):
+        copy = pltpu.make_async_copy(out.at[i, h], ref.at[:, h * HD : (h + 1) * HD], store.at[i, h])
+        copy.start()
+        stores.append(copy)
 
     def spread_columns(h):
         send(ew_out.at[h, 0], ew_in.at[h, 0], dew_s.at[h, 0], dew_r.at[h, 0], west)
@@ -299,25 +304,28 @@
             ew_out[h, 0, kv] = dwin[h, kv, 0].astype(jnp.bfloat16)
             ew_out[h, 1, kv] = dwin[h, kv, 3].astype(jnp.bfloat16)
         spread_columns(h)
-        dq_ref[:, lanes] = lax.dot_general(
+        out[0, h] = lax.dot_general(
             grad_s[...], keys, FIRST, preferred_element_type=jnp.float32
         ).astype(jnp.bfloat16)
+        leave(0, dq_hbm, h)
 
     def finish(h):
-        lanes = slice(h * HD, (h + 1) * HD)
         wait_recv(ns_in.at[h, 0], dns_r.at[h, 0])
         wait_recv(ns_in.at[h, 1], dns_r.at[h, 1])
-        for kv, ref in enumerate((dk_ref, dv_ref)):
+        for kv, ref in enumerate((dk_hbm, dv_hbm)):
             halves = []
             for i in range(2):
                 upper = dwin[h, kv, 1 + i, STRIP : 2 * STRIP] + ns_in[h, 1, kv, i].astype(jnp.float32)
                 lower = dwin[h, kv, 1 + i, 2 * STRIP : 3 * STRIP] + ns_in[h, 0, kv, i].astype(jnp.float32)
                 halves.append(jnp.concatenate([upper, lower], axis=0).reshape(16, 8, HD))
-            ref[:, lanes] = jnp.stack(halves, axis=1).reshape(TOK, HD).astype(jnp.bfloat16)
+            out[1 + kv, h] = jnp.stack(halves, axis=1).reshape(TOK, HD).astype(jnp.bfloat16)
+            leave(1 + kv, ref, h)
 
     softmax(0)
+    halo_columns(1)
     backward(0)
     softmax(1)
+    halo_columns(2)
     spread_rows(0)
     backward(1)
     softmax(2)
@@ -329,6 +337,8 @@
 
     for copy in sent:
         copy.wait_send()
+    for copy in stores:
+        copy.wait()
     for hi in range(2):
         device = scatter_to[hi]
         mine = (device[0] == t) & (device[1] == mp)
@@ -344,20 +354,31 @@
             @pl.when(jnp.logical_not(mine))
             def _():
                 copy.wait_send()
+
+
+def hand_over(a, b, c, a_out, b_out, c_out, held, sem):
+    into = [pltpu.make_async_copy(src, held.at[i], sem.at[0, i]) for i, src in enumerate((a, b, c))]
+    out_of = [pltpu.make_async_copy(held.at[i], dst, sem.at[1, i]) for i, dst in enumerate((a_out, b_out, c_out))]
+    for copy in into:
+        copy.start()
+    for first, second in zip(into, out_of):
+        first.wait()
+        second.start()
+    for copy in out_of:
+        copy.wait()
 
 
 def shards(query, key, value, grad_y, w_out):
     bf16, f32 = jnp.bfloat16, jnp.float32
     dma = pltpu.SemaphoreType.DMA
     out = jax.ShapeDtypeStruct(query.shape, bf16)
-    vmem = pl.BlockSpec(memory_space=pltpu.VMEM)
     hbm = pl.BlockSpec(memory_space=pltpu.HBM)
-    return pl.pallas_call(
+    grads = pl.pallas_call(
         kernel,
         name="tiled_attention_backward",
         out_shape=(out, out, out),
         in_specs=[hbm] * 5,
-        out_specs=(vmem,) * 3,
+        out_specs=(hbm,) * 3,
         scratch_shapes=[
             pltpu.VMEM((HEADS_DEV, 2, 4, 256, HD), bf16),
             pltpu.VMEM((32, HEADS_DEV * HD), bf16),
@@ -379,6 +400,7 @@
             pltpu.VMEM(key.shape, bf16),
             pltpu.VMEM(value.shape, bf16),
             pltpu.VMEM(w_out.shape, bf16),
+            pltpu.VMEM((3, HEADS_DEV, TOK, HD), bf16),
             dma((HEADS_DEV, 2)), dma((HEADS_DEV, 2)),
             dma((HEADS_DEV, 2)), dma((HEADS_DEV, 2)),
             dma((2,)), dma((2,)),
@@ -389,11 +411,21 @@
             dma((HEADS_DEV, 2)), dma((HEADS_DEV, 2)),
             dma((HEADS_DEV, 2)), dma((HEADS_DEV, 2)),
             dma((5,)),
+            dma((3, HEADS_DEV)),
         ],
         compiler_params=pltpu.CompilerParams(
             collective_id=0, has_side_effects=True, vmem_limit_bytes=60 * 1024 * 1024
         ),
     )(query, key, value, grad_y, w_out)
+    return pl.pallas_call(
+        hand_over,
+        name="hand_over",
+        out_shape=(out, out, out),
+        in_specs=[hbm] * 3,
+        out_specs=(hbm,) * 3,
+        scratch_shapes=[pltpu.VMEM((3,) + query.shape, bf16), dma((2, 3))],
+        compiler_params=pltpu.CompilerParams(vmem_limit_bytes=60 * 1024 * 1024),
+    )(*grads)
 
 
 def solution(mesh):

time: 81.1 us -> 77.9 us (0.961)
  local copies, waits for them, and re-layouts: 3.34 us -> 0 us
    unnamed x7 -> x0, local copies, waits for them, and re-layouts: 3.34 us -> none
    pallas_call x0 -> x1, Pallas kernels: none -> 1.84 us  [shards(): pl.pallas_call(hand_over, name='hand_over', out_shape=(out, out, out), in...]
    pallas_call x1, Pallas kernels: 76 us -> 74.1 us  [shards(): pl.pallas_call(kernel, name='tiled_attention_backward', out_shape=(out, o...]
where the time goes in v4:
time: 77.9 us; the launch traced here: 76.6 us
  Pallas kernels  76 us (98%)
    pallas_call x1, Pallas kernels, shards(): pl.pallas_call(kernel, name='tiled_attention_backward', out_shape=(out, o...  74.1 us
    pallas_call x1, Pallas kernels, shards(): pl.pallas_call(hand_over, name='hand_over', out_shape=(out, out, out), in...  1.84 us

profile of v4, /device:TPU:57, one launch (start us, length us, event | category | flops | bytes accessed | tf_op | source)
XLA Modules:
  0.0 76.6 jit_solution(6355919739837768195)
XLA Ops:
  0.6 74.1 %tiled_attention_backward.1 = (bf16[256,384]{1,0:T(8,128)(2,1)}, bf16[256,384]{1,0:T(8,128)(2,1)}, bf16[256,384]{1,0:T(8,128)(2,1)}) custom-call(bf16[256,384]{1,0:T(8,128)(2,1)} %q_hbm.1, bf16[256,384]{1,0:T(8,128)(2,1)} %k_hbm.1, bf16[256,384]{1,0:T(8,128)(2,1)} %v_hbm.1, bf16[256,768]{1,0:T(8,128)(2,1)} %g_hbm.1, bf16[24,384]{1,0:T(8,128)(2,1)} %w_hbm.1), custom_call_target="tpu_custom_call" | custom-call | tf_op jit(solution)/shard_map/tiled_attention_backward/pallas_call | solution.py:376
  74.8 1.8 %hand_over.1 = (bf16[256,384]{1,0:T(8,128)(2,1)}, bf16[256,384]{1,0:T(8,128)(2,1)}, bf16[256,384]{1,0:T(8,128)(2,1)}) custom-call(bf16[256,384]{1,0:T(8,128)(2,1)} %get-tuple-element.6.a, bf16[256,384]{1,0:T(8,128)(2,1)} %get-tuple-element.7.b, bf16[256,384]{1,0:T(8,128)(2,1)} %get-tuple-element.8.c), custom_call_target="tpu_custom_call" | custom-call | tf_op jit(solution)/shard_map/hand_over/pallas_call | solution.py:420

commit v5 on v3

--- a/solution.py
+++ b/solution.py
@@ -159,7 +159,17 @@
 
     halo_rows(0)
     halo_rows(1)
-    halo_rows(2)
+
+    key_at = lax.broadcasted_iota(jnp.int32, (KEYS, CHUNK), 0)
+    group = key_at // 256
+    key_row = lax.rem(key_at, 256) // 8
+    valid = (
+        ((group > 0) | (col > 0))
+        & ((group < 3) | (col < COLUMNS - 1))
+        & ((key_row >= 8) | (row > 0))
+        & ((key_row < 24) | (row < ROWS - 1))
+    )
+    bias[...] = jnp.where(valid, 0.0, -1e30)
 
     for c in range(2):
         wait_recv(stage.at[c], wsc_r.at[c])
@@ -185,6 +195,7 @@
         wait_recv(theirs, wy_r.at[d])
         for e in x_order:
             send(theirs, theirs, wx_s.at[d, e], wx_r.at[d, e], x_peer(e))
+    halo_rows(2)
 
     wait_recv(near_g, g_r.at[0])
     send(near_g, near_g, g_s.at[2], g_r.at[2], other)
@@ -228,19 +239,7 @@
     share(2)
 
     halo_columns(0)
-    halo_columns(1)
-    halo_columns(2)
     loads[4].wait()
-    key_at = lax.broadcasted_iota(jnp.int32, (KEYS, CHUNK), 0)
-    group = key_at // 256
-    key_row = lax.rem(key_at, 256) // 8
-    valid = (
-        ((group > 0) | (col > 0))
-        & ((group < 3) | (col < COLUMNS - 1))
-        & ((key_row >= 8) | (row > 0))
-        & ((key_row < 24) | (row < ROWS - 1))
-    )
-    bias[...] = jnp.where(valid, 0.0, -1e30)
 
     def softmax(h):
         wait_recv(win.at[h, :, 3], kvew_r.at[h, 0])
@@ -304,7 +303,6 @@
         ).astype(jnp.bfloat16)
 
     def finish(h):
-        lanes = slice(h * HD, (h + 1) * HD)
         wait_recv(ns_in.at[h, 0], dns_r.at[h, 0])
         wait_recv(ns_in.at[h, 1], dns_r.at[h, 1])
         for kv, ref in enumerate((dk_ref, dv_ref)):
@@ -313,21 +311,23 @@
                 upper = dwin[h, kv, 1 + i, STRIP : 2 * STRIP] + ns_in[h, 1, kv, i].astype(jnp.float32)
                 lower = dwin[h, kv, 1 + i, 2 * STRIP : 3 * STRIP] + ns_in[h, 0, kv, i].astype(jnp.float32)
                 halves.append(jnp.concatenate([upper, lower], axis=0).reshape(16, 8, HD))
-            ref[:, lanes] = jnp.stack(halves, axis=1).reshape(TOK, HD).astype(jnp.bfloat16)
+            ref[:, h * HD : (h + 1) * HD] = jnp.stack(halves, axis=1).reshape(TOK, HD).astype(jnp.bfloat16)
 
     softmax(0)
+    halo_columns(1)
     backward(0)
     softmax(1)
+    halo_columns(2)
     spread_rows(0)
     backward(1)
     softmax(2)
     spread_rows(1)
     backward(2)
     spread_rows(2)
-    for h in range(HEADS_DEV):
+    for h in range(HEADS_DEV - 1):
         finish(h)
 
-    for copy in sent:
+    for copy in sent[:-2]:
         copy.wait_send()
     for hi in range(2):
         device = scatter_to[hi]
@@ -345,17 +345,33 @@
             def _():
                 copy.wait_send()
 
+    finish(HEADS_DEV - 1)
+    for copy in sent[-2:]:
+        copy.wait_send()
+
+
+def hand_over(a, b, c, a_out, b_out, c_out, sem):
+    copies = [
+        pltpu.make_async_copy(src, dst, sem.at[i])
+        for i, (src, dst) in enumerate(((a, a_out), (b, b_out), (c, c_out)))
+    ]
+    for copy in copies:
+        copy.start()
+    for copy in copies:
+        copy.wait()
+
 
 def shards(query, key, value, grad_y, w_out):
     bf16, f32 = jnp.bfloat16, jnp.float32
     dma = pltpu.SemaphoreType.DMA
     out = jax.ShapeDtypeStruct(query.shape, bf16)
+    held = pltpu.VMEM(query.shape, bf16)
     vmem = pl.BlockSpec(memory_space=pltpu.VMEM)
     hbm = pl.BlockSpec(memory_space=pltpu.HBM)
-    return pl.pallas_call(
+    grads = pl.pallas_call(
         kernel,
         name="tiled_attention_backward",
-        out_shape=(out, out, out),
+        out_shape=(held, held, held),
         in_specs=[hbm] * 5,
         out_specs=(vmem,) * 3,
         scratch_shapes=[
@@ -394,6 +410,14 @@
             collective_id=0, has_side_effects=True, vmem_limit_bytes=60 * 1024 * 1024
         ),
     )(query, key, value, grad_y, w_out)
+    return pl.pallas_call(
+        hand_over,
+        name="hand_over",
+        out_shape=(out, out, out),
+        in_specs=[vmem] * 3,
+        out_specs=(hbm,) * 3,
+        scratch_shapes=[dma((3,))],
+    )(*(pltpu.with_memory_space_constraint(g, pltpu.VMEM) for g in grads))
 
 
 def solution(mesh):

time: 81.1 us -> 76 us (0.937); the launches traced: 80 us -> 75.8 us
  local copies, waits for them, and re-layouts: 3.34 us -> 0 us
  Pallas kernels: 76 us -> 75.1 us
    unnamed x7 -> x0, local copies, waits for them, and re-layouts: 3.34 us -> none
    pallas_call x1 -> x2, Pallas kernels: 76 us -> 75.1 us  [the longest x1 74.3 us: shards(): pl.pallas_call(kernel, name='tiled_attention_backward', out_shape=(held,...]
where the time goes in v5:
time: 76 us; the launch traced here: 75.8 us
  Pallas kernels  75.1 us (99%)
    pallas_call x1, Pallas kernels, shards(): pl.pallas_call(kernel, name='tiled_attention_backward', out_shape=(held,...  74.3 us

profile of v5, /device:TPU:57, one launch (start us, length us, event | category | flops | bytes accessed | tf_op | source)
XLA Modules:
  0.0 75.8 jit_solution(2695920003913905563)
XLA Ops:
  0.6 74.3 %tiled_attention_backward.1 = (bf16[256,384]{1,0:T(8,128)(2,1)S(1)}, bf16[256,384]{1,0:T(8,128)(2,1)S(1)}, bf16[256,384]{1,0:T(8,128)(2,1)S(1)}) custom-call(bf16[256,384]{1,0:T(8,128)(2,1)} %q_hbm.1, bf16[256,384]{1,0:T(8,128)(2,1)} %k_hbm.1, bf16[256,384]{1,0:T(8,128)(2,1)} %v_hbm.1, bf16[256,768]{1,0:T(8,128)(2,1)} %g_hbm.1, bf16[24,384]{1,0:T(8,128)(2,1)} %w_hbm.1), custom_call_target="tpu_custom_call" | custom-call | tf_op jit(solution)/shard_map/tiled_attention_backward/pallas_call | solution.py:371
  75.0 0.8 %hand_over.1 = (bf16[256,384]{1,0:T(8,128)(2,1)}, bf16[256,384]{1,0:T(8,128)(2,1)}, bf16[256,384]{1,0:T(8,128)(2,1)}) custom-call(bf16[256,384]{1,0:T(8,128)(2,1)S(1)} %get-tuple-element.6.a, bf16[256,384]{1,0:T(8,128)(2,1)S(1)} %get-tuple-element.7.b, bf16[256,384]{1,0:T(8,128)(2,1)S(1)} %get-tuple-element.8.c), custom_call_target="tpu_custom_call" | custom-call | tf_op jit(solution)/shard_map/hand_over/pallas_call | solution.py:413

commit v6 on v5

--- a/solution.py
+++ b/solution.py
@@ -41,7 +41,7 @@
 def kernel(
     q_hbm, k_hbm, v_hbm, g_hbm, w_hbm, dq_ref, dk_ref, dv_ref,
     win, wpad, stage, wbuf, gall, part, arrived, bias, prob, grad_s, prob_low, dwin,
-    ew_out, ew_in, ns_out, ns_in, q, k, v, w,
+    ew_out, ew_in, ns_out, ns_in, q, k, v,
     kvns_s, kvns_r, kvew_s, kvew_r, wsc_s, wsc_r, g_s, g_r, wy_s, wy_r, wx_s, wx_r,
     rs_s, rs_r, dew_s, dew_r, dns_s, dns_r, load,
 ):
@@ -86,14 +86,12 @@
 
     loads = []
     for i, (src, dst) in enumerate(
-        ((w_hbm, w), (k_hbm, k), (v_hbm, v), (g_hbm, gall.at[side, core]), (q_hbm, q))
+        ((w_hbm, wpad), (k_hbm, k), (v_hbm, v), (g_hbm, gall.at[side, core]), (q_hbm, q))
     ):
         loads.append(pltpu.make_async_copy(src, dst, load.at[i]))
         loads[-1].start()
 
     loads[0].wait()
-    wpad[0:24, :] = w[...]
-    wpad[24:32, :] = jnp.zeros((8, HEADS_DEV * HD), jnp.bfloat16)
     loads[1].wait()
     loads[2].wait()
     for h in range(HEADS_DEV):
@@ -394,7 +392,6 @@
             pltpu.VMEM(query.shape, bf16),
             pltpu.VMEM(key.shape, bf16),
             pltpu.VMEM(value.shape, bf16),
-            pltpu.VMEM(w_out.shape, bf16),
             dma((HEADS_DEV, 2)), dma((HEADS_DEV, 2)),
             dma((HEADS_DEV, 2)), dma((HEADS_DEV, 2)),
             dma((2,)), dma((2,)),
@@ -409,7 +406,7 @@
         compiler_params=pltpu.CompilerParams(
             collective_id=0, has_side_effects=True, vmem_limit_bytes=60 * 1024 * 1024
         ),
-    )(query, key, value, grad_y, w_out)
+    )(query, key, value, grad_y, jnp.pad(w_out, ((0, 8), (0, 0))))
     return pl.pallas_call(
         hand_over,
         name="hand_over",

time: 76 us -> 77.4 us (1.018)
  local copies, waits for them, and re-layouts: 0 us -> 1.33 us
    pad x0 -> x1, local copies, waits for them, and re-layouts: none -> 1.33 us  [shards(): jnp.pad(w_out, ((0, 8), (0, 0)))]
where the time goes in v6:
time: 77.4 us; the launch traced here: 77.1 us
  Pallas kernels  75.1 us (97%)
  local copies, waits for them, and re-layouts  1.33 us (2%)
    pallas_call x1, Pallas kernels, shards(): pl.pallas_call(kernel, name='tiled_attention_backward', out_shape=(held,...  74.3 us

profile of v6, /device:TPU:57, one launch (start us, length us, event | category | flops | bytes accessed | tf_op | source)
XLA Modules:
  0.0 77.1 jit_solution(15388373947237225133)
XLA Ops:
  0.6 1.3 %pad.4.w_hbm = bf16[32,384]{1,0:T(8,128)(2,1)} pad(bf16[24,384]{1,0:T(8,128)(2,1)} %param.9, bf16[]{:T(256)} %constant.2.clone.1), padding=0_8x0_0 | pad | bytes 43010 | tf_op jit(solution)/shard_map/jit(_pad)/pad | solution.py:409
  2.0 74.3 %tiled_attention_backward.1 = (bf16[256,384]{1,0:T(8,128)(2,1)S(1)}, bf16[256,384]{1,0:T(8,128)(2,1)S(1)}, bf16[256,384]{1,0:T(8,128)(2,1)S(1)}) custom-call(bf16[256,384]{1,0:T(8,128)(2,1)} %q_hbm.1, bf16[256,384]{1,0:T(8,128)(2,1)} %k_hbm.1, bf16[256,384]{1,0:T(8,128)(2,1)} %v_hbm.1, bf16[256,768]{1,0:T(8,128)(2,1)} %g_hbm.1, bf16[32,384]{1,0:T(8,128)(2,1)} %pad.4.w_hbm), custom_call_target="tpu_custom_call" | custom-call | tf_op jit(solution)/shard_map/tiled_attention_backward/pallas_call | solution.py:369
  76.3 0.8 %hand_over.1 = (bf16[256,384]{1,0:T(8,128)(2,1)}, bf16[256,384]{1,0:T(8,128)(2,1)}, bf16[256,384]{1,0:T(8,128)(2,1)}) custom-call(bf16[256,384]{1,0:T(8,128)(2,1)S(1)} %get-tuple-element.6.a, bf16[256,384]{1,0:T(8,128)(2,1)S(1)} %get-tuple-element.7.b, bf16[256,384]{1,0:T(8,128)(2,1)S(1)} %get-tuple-element.8.c), custom_call_target="tpu_custom_call" | custom-call | tf_op jit(solution)/shard_map/hand_over/pallas_call | solution.py:410

commit v7 on v6

--- a/solution.py
+++ b/solution.py
@@ -39,7 +39,7 @@
 
 
 def kernel(
-    q_hbm, k_hbm, v_hbm, g_hbm, w_hbm, dq_ref, dk_ref, dv_ref,
+    q_hbm, k_hbm, v_hbm, g_hbm, w_ref, dq_ref, dk_ref, dv_ref,
     win, wpad, stage, wbuf, gall, part, arrived, bias, prob, grad_s, prob_low, dwin,
     ew_out, ew_in, ns_out, ns_in, q, k, v,
     kvns_s, kvns_r, kvew_s, kvew_r, wsc_s, wsc_r, g_s, g_r, wy_s, wy_r, wx_s, wx_r,
@@ -86,21 +86,22 @@
 
     loads = []
     for i, (src, dst) in enumerate(
-        ((w_hbm, wpad), (k_hbm, k), (v_hbm, v), (g_hbm, gall.at[side, core]), (q_hbm, q))
+        ((k_hbm, k), (v_hbm, v), (g_hbm, gall.at[side, core]), (q_hbm, q))
     ):
         loads.append(pltpu.make_async_copy(src, dst, load.at[i]))
         loads[-1].start()
 
+    wpad[0:24, :] = w_ref[...]
+    wpad[24:32, :] = jnp.zeros((8, HEADS_DEV * HD), jnp.bfloat16)
     loads[0].wait()
     loads[1].wait()
-    loads[2].wait()
     for h in range(HEADS_DEV):
         lanes = slice(h * HD, (h + 1) * HD)
         for kv, ref in enumerate((k, v)):
             halves = to_halves(ref[:, lanes])
             for i in range(2):
                 win[h, kv, 1 + i, STRIP : STRIP + 128, :] = halves[i]
-    loads[3].wait()
+    loads[2].wait()
     pl.semaphore_wait(barrier, len(greeted))
 
     def remote(src, dst, send, recv, device):
@@ -237,7 +238,7 @@
     share(2)
 
     halo_columns(0)
-    loads[4].wait()
+    loads[3].wait()
 
     def softmax(h):
         wait_recv(win.at[h, :, 3], kvew_r.at[h, 0])
@@ -370,7 +371,7 @@
         kernel,
         name="tiled_attention_backward",
         out_shape=(held, held, held),
-        in_specs=[hbm] * 5,
+        in_specs=[hbm] * 4 + [vmem],
         out_specs=(vmem,) * 3,
         scratch_shapes=[
             pltpu.VMEM((HEADS_DEV, 2, 4, 256, HD), bf16),
@@ -401,12 +402,12 @@
             dma((HEADS_DEV, 2)), dma((HEADS_DEV, 2)),
             dma((HEADS_DEV, 2)), dma((HEADS_DEV, 2)),
             dma((HEADS_DEV, 2)), dma((HEADS_DEV, 2)),
-            dma((5,)),
+            dma((4,)),
         ],
         compiler_params=pltpu.CompilerParams(
             collective_id=0, has_side_effects=True, vmem_limit_bytes=60 * 1024 * 1024
         ),
-    )(query, key, value, grad_y, jnp.pad(w_out, ((0, 8), (0, 0))))
+    )(query, key, value, grad_y, pltpu.with_memory_space_constraint(w_out, pltpu.VMEM))
     return pl.pallas_call(
         hand_over,
         name="hand_over",

time: 77.4 us -> 76.7 us (level)
    pad x1 -> x0, local copies, waits for them, and re-layouts: 1.33 us -> none  [shards(): jnp.pad(w_out, ((0, 8), (0, 0)))]
where the time goes in v7:
time: 76.7 us; the launch traced here: 76.5 us
  Pallas kernels  75.1 us (98%)
    pallas_call x1, Pallas kernels, shards(): pl.pallas_call(kernel, name='tiled_attention_backward', out_shape=(held,...  74.3 us

profile of v7, /device:TPU:57, one launch (start us, length us, event | category | flops | bytes accessed | tf_op | source)
XLA Modules:
  0.0 76.5 jit_solution(14158442574951046314)
XLA Ops:
  0.6 0.0 copy-start
  0.6 0.7 copy-done
  1.4 74.3 %tiled_attention_backward.1 = (bf16[256,384]{1,0:T(8,128)(2,1)S(1)}, bf16[256,384]{1,0:T(8,128)(2,1)S(1)}, bf16[256,384]{1,0:T(8,128)(2,1)S(1)}) custom-call(bf16[256,384]{1,0:T(8,128)(2,1)} %q_hbm.1, bf16[256,384]{1,0:T(8,128)(2,1)} %k_hbm.1, bf16[256,384]{1,0:T(8,128)(2,1)} %v_hbm.1, bf16[256,768]{1,0:T(8,128)(2,1)} %g_hbm.1, bf16[24,384]{1,0:T(8,128)(2,1)S(1)} %copy-done), custom_call_target="tpu_custom_call" | custom-call | tf_op jit(solution)/shard_map/tiled_attention_backward/pallas_call | solution.py:370
  75.7 0.8 %hand_over.1 = (bf16[256,384]{1,0:T(8,128)(2,1)}, bf16[256,384]{1,0:T(8,128)(2,1)}, bf16[256,384]{1,0:T(8,128)(2,1)}) custom-call(bf16[256,384]{1,0:T(8,128)(2,1)S(1)} %get-tuple-element.6.a, bf16[256,384]{1,0:T(8,128)(2,1)S(1)} %get-tuple-element.7.b, bf16[256,384]{1,0:T(8,128)(2,1)S(1)} %get-tuple-element.8.c), custom_call_target="tpu_custom_call" | custom-call | tf_op jit(solution)/shard_map/hand_over/pallas_call | solution.py:411
Async XLA Ops:
  0.6 0.7 copy-start
